TPU v7x, 256 devices: a whole 4x4x8 slice. The times are simulated.
256 devices in a mesh: section: 4 (over x), tile: 64 (over z, y, core).
Axes of the slice: x: 4, y: 4, z: 8, core: 2. Of those that a mesh axis runs over, the one named last changes fastest.
Arguments:
- latents: bfloat16 [16, 64, 4, 24, 384], P('section', 'tile'), may hold values from -6 to 6
- frame_counts: int32 [4], replicated, may hold values from 2 to 4, as said below
- norm_gain: float32 [384], replicated, may hold values from 0.1 to 1.9
- conv_weight: bfloat16 [3, 3, 3, 384, 384], replicated, may hold values from -0.0625 to 0.0625
- up_weight: bfloat16 [3, 3, 384, 192], replicated, may hold values from -0.109375 to 0.109375
- pixel_grad: bfloat16 [16, 64, 8, 24, 384], P('section', 'tile'), may hold values from -6 to 6
Outputs:
- decoded: bfloat16 [16, 64, 8, 24, 384], P('section', 'tile')
- latent_grad: float32 [16, 64, 4, 24, 384], P('section', 'tile')
Inputs may be any that keep to these rules, and one draw needn't show every extreme that they name: `frame_counts`: every group has at least two frames; some group is full in every draw.
All inputs are finite; a program needn't handle non-finite values.
Results may differ from a plain program's by a relative error of at most 0.0058.
Values may be sent and summed in bfloat16 or wider, within the bound.
No kernel may reach another device: no remote copies, remote signals or barrier semaphores. Data moves between devices by JAX's collectives and lax.ppermute only.
A program may use at most 64 MiB of HBM per device.

v0:
```python
import functools

import jax
import jax.numpy as jnp
from jax import lax
from jax.experimental import pallas as pl
from jax.experimental.pallas import tpu as pltpu
from jax.sharding import PartitionSpec as P

GCOL = 4
EPS = 1e-06
F, BR, BW, C, CP = 4, 4, 24, 384, 32
BF, F32 = jnp.bfloat16, jnp.float32
NT = (((1,), (1,)), ((), ()))
VM = pl.BlockSpec(memory_space=pltpu.VMEM)
SM = pl.BlockSpec(memory_space=pltpu.SMEM)
ANY = pl.BlockSpec(memory_space=pl.ANY)


def place_of(axis_sizes):
    sections, tiles = axis_sizes
    at = lax.rem(lax.axis_index("tile") + GCOL + 1, tiles)
    row, col = lax.div(at, GCOL), lax.rem(at, GCOL)
    section = lax.axis_index("section")
    return dict(
        section=section,
        up=row > 0,
        down=row < tiles // GCOL - 1,
        left=col > 0,
        right=col < GCOL - 1,
        before=section > 0,
        after=section < sections - 1,
    )


def column_mask(where, width, valid):
    column = lax.broadcasted_iota(jnp.int32, (1, CP, C), 1)
    own = column < BW
    right = (column >= BW) & (column < BW + valid) & where["right"]
    left = (column >= CP - valid) & where["left"]
    return own | right | left


def activate(values, gain):
    scale = lax.rsqrt(jnp.mean(values * values, axis=-1, keepdims=True) + EPS)
    normed = values * scale * gain
    return normed * jax.nn.sigmoid(normed)


def shifted(x, by):
    return pltpu.roll(x, (-by) % CP, axis=x.ndim - 2)


def acts_kernel(sizes, lat, halo, gain, out):
    where = place_of(sizes)
    mask = column_mask(where, C, 2)
    g = gain[...].reshape(1, 1, C)
    for f in range(F):
        whole = jnp.concatenate(
            [lat[f].astype(F32), halo[f, 0:BR].astype(F32)], axis=1
        )
        out[f] = jnp.where(mask, activate(whole, g), 0.0).astype(BF)


def grad_hidden_kernel(sizes, counts, pg, halo, upw, out, parts, acc):
    where = place_of(sizes)
    length = counts[where["section"]]
    mask = column_mask(where, C, 2)
    low = lax.broadcasted_iota(jnp.int32, (1, CP, C), 2) < C // 2
    for f in range(F):
        for r in range(0, 2 * BR, 2):
            whole = jnp.concatenate(
                [pg[f, r : r + 2].astype(F32), halo[f, BR + r : BR + r + 2].astype(F32)], axis=1
            )
            whole = jnp.where(mask & (f < length), whole, 0.0)
            mix = jnp.where(low, shifted(whole, 1), shifted(whole, -1))
            for k in range(2):
                rows = slice((r // 2) * CP, (r // 2 + 1) * CP)
                parts[k, f, rows, 0:C] = whole[k].astype(BF)
                parts[k, f, rows, C : 2 * C] = mix[k].astype(BF)
    even = parts[0].reshape(F * BR * CP, 2 * C)
    odd = parts[1].reshape(F * BR * CP, 2 * C)

    def term(x, w):
        return lax.dot_general(x, upw[w], NT, preferred_element_type=F32).reshape(F, BR * CP, C)

    acc[:, CP : 5 * CP] = term(even, 0) + term(odd, 2)
    acc[:, 0:CP] = jnp.zeros((F, CP, C), F32)
    acc[:, 5 * CP : 6 * CP] = jnp.zeros((F, CP, C), F32)
    acc[:, 0 : 4 * CP] += term(even, 1)
    acc[:, 2 * CP : 6 * CP] += term(odd, 3)
    inner = column_mask(where, C, 1)
    for f in range(F):
        value = acc[f].reshape(6, CP, C)
        row = lax.broadcasted_iota(jnp.int32, (6, CP, C), 0)
        keep = inner & ((row > 0) | where["up"]) & ((row < 5) | where["down"])
        out[f] = jnp.where(keep, value, 0.0).astype(BF)


def back_kernel(gh, weight, acc_out, early_out, wt, cells, acc, sems):
    copies = {}
    for dt in (2, 1, 0):
        for dr in range(3):
            for dc in range(3):
                copy = pltpu.make_async_copy(
                    weight.at[dt, dr, dc],
                    wt.at[dt, dr * C : (dr + 1) * C, dc * C : (dc + 1) * C],
                    sems.at[dt * 9 + dr * 3 + dc],
                )
                copy.start()
                copies[dt, dr, dc] = copy
    for f in range(F):
        value = gh[f].astype(F32)
        for dc in range(3):
            moved = value if dc == 1 else shifted(value, 1 - dc)
            cells[f, :, dc * C : (dc + 1) * C] = moved[:, 0:BW].reshape(6 * BW, C).astype(BF)
    acc[...] = jnp.zeros(acc.shape, F32)
    left = cells[...].reshape(F * 6 * BW, 3 * C)
    for dt in (2, 1, 0):
        for dr in range(3):
            for dc in range(3):
                copies[dt, dr, dc].wait()
        product = lax.dot_general(left, wt[dt], NT, preferred_element_type=F32)
        for f in range(F):
            for dr in range(3):
                acc[f + dt, dr * BW : (dr + 6) * BW] += product[
                    f * 6 * BW : (f + 1) * 6 * BW, dr * C : (dr + 1) * C
                ]
    early_out[...] = acc[0:2].astype(BF)
    acc_out[...] = acc[2:6]


def edge_frames_kernel(sizes, counts, own, above, below, out):
    where = place_of(sizes)
    length = counts[where["section"]]
    for k in range(2):
        f = length - 2 + k
        out[k, 0:2] = jnp.where(where["up"], above[f], jnp.zeros((2, CP, C), BF))
        out[k, 2:6] = own[f]
        out[k, 6:8] = jnp.where(where["down"], below[f], jnp.zeros((2, CP, C), BF))


def side_by_side(x, rows, cells, f):
    for dc in range(3):
        moved = x if dc == 1 else shifted(x, dc - 1)
        count = x.shape[0] * CP
        cells[f, rows * CP : rows * CP + count, dc * C : (dc + 1) * C] = moved.reshape(
            count, C
        ).astype(BF)


def forward_kernel(sizes, own, above, below, weight, acc_out, wt, cells, sems):
    copies = {}
    for dt in (2, 1, 0):
        for dr in range(3):
            copy = pltpu.make_async_copy(weight.at[dt, dr], wt.at[dt * 3 + dr], sems.at[dt * 3 + dr])
            copy.start()
            copies[dt, dr] = copy
    where = place_of(sizes)
    for f in range(F):
        side_by_side(jnp.where(where["up"], above[f].astype(F32), 0.0), 0, cells, f)
        side_by_side(own[f].astype(F32), 2, cells, f)
        side_by_side(jnp.where(where["down"], below[f].astype(F32), 0.0), 6, cells, f)
    for dt in (2, 1, 0):
        count = F - (2 - dt)
        total = None
        for dr in range(3):
            copies[dt, dr].wait()
            left = cells[0:count, dr * CP : (dr + 6) * CP].reshape(count * 6 * CP, 3 * C)
            term = jnp.dot(left, wt[dt * 3 + dr], preferred_element_type=F32)
            total = term if total is None else total + term
        total = total.reshape(count, 6 * CP, C)
        if dt == 2:
            acc_out[...] = total
        else:
            acc_out[2 - dt : F] += total


def decode_kernel(sizes, counts, part, prior, weight, upw, out, wt, cells, pairs, sems):
    copies = {}
    for dt in (0, 1):
        for dr in range(3):
            copy = pltpu.make_async_copy(weight.at[dt, dr], wt.at[dt * 3 + dr], sems.at[dt * 3 + dr])
            copy.start()
            copies[dt, dr] = copy
    where = place_of(sizes)
    length = counts[where["section"]]
    for k in range(2):
        side_by_side(jnp.where(where["before"], prior[k].astype(F32), 0.0), 0, cells, k)

    def term(first, count, dt):
        total = None
        for dr in range(3):
            left = cells[first : first + count, dr * CP : (dr + 6) * CP].reshape(count * 6 * CP, 3 * C)
            value = jnp.dot(left, wt[dt * 3 + dr], preferred_element_type=F32)
            total = value if total is None else total + value
        return total.reshape(count, 6 * CP, C)

    for dr in range(3):
        copies[0, dr].wait()
    early = part[0:2] + term(0, 2, 0)
    for dr in range(3):
        copies[1, dr].wait()
    late = term(1, 1, 1)
    inner = column_mask(where, C, 1)
    row = lax.broadcasted_iota(jnp.int32, (6, CP, C), 0)
    keep = inner & ((row > 0) | where["up"]) & ((row < 5) | where["down"])
    for f in range(F):
        value = part[f] if f >= 2 else early[f]
        if f == 0:
            value = value + late[0]
        hidden = jnp.where(keep, value.reshape(6, CP, C), 0.0).reshape(6 * CP, C).astype(BF)
        pairs[0, f, :, 0:C] = hidden[CP : 5 * CP]
        pairs[0, f, :, C : 2 * C] = hidden[0 : 4 * CP]
        pairs[1, f, :, 0:C] = hidden[CP : 5 * CP]
        pairs[1, f, :, C : 2 * C] = hidden[2 * CP : 6 * CP]
    low = lax.broadcasted_iota(jnp.int32, (1, CP, C), 2) < C // 2
    for k in range(2):
        rows = jnp.dot(
            pairs[k].reshape(F * 4 * CP, 2 * C),
            upw[2 * k : 2 * k + 2].reshape(2 * C, 2 * C),
            preferred_element_type=F32,
        )
        for f in range(F):
            whole = rows[f * 4 * CP : (f + 1) * 4 * CP].reshape(4, CP, 2 * C)
            side = whole[:, :, C : 2 * C]
            mix = jnp.where(low, shifted(side, -1), shifted(side, 1))
            value = jnp.where(f < length, whole[:, :, 0:C] + mix, 0.0)[:, 0:BW].astype(BF)
            for r in range(BR):
                out[f, 2 * r + k] = value[r]


def later_group_kernel(sizes, counts, acc, later, top, bottom, own, total):
    where = place_of(sizes)
    length = counts[where["section"]]
    total[...] = acc[...]
    for k in range(2):
        f = length - 2 + k
        total[f] += jnp.where(where["after"], later[k].astype(F32), 0.0)
    top[...] = total[:, 0 : 2 * BW].astype(BF)
    bottom[...] = total[:, 6 * BW : 8 * BW].astype(BF)
    own[...] = total[:, 2 * BW : 6 * BW]


def latent_grad_kernel(sizes, counts, lat, gain, own, above, below, out):
    where = place_of(sizes)
    length = counts[where["section"]]
    g = gain[...].reshape(1, 1, C)
    for f in range(F):
        x = lat[f].astype(F32)
        upper = own[f, 0 : 2 * BW] + jnp.where(where["up"], above[f].astype(F32), 0.0)
        lower = own[f, 2 * BW : 4 * BW] + jnp.where(where["down"], below[f].astype(F32), 0.0)
        grad = jnp.concatenate([upper, lower], 0).reshape(BR, BW, C)
        scale = lax.rsqrt(jnp.mean(x * x, axis=-1, keepdims=True) + EPS)
        unit = x * scale
        v = unit * g
        s = jax.nn.sigmoid(v)
        t = grad * (s + v * s * (1.0 - s)) * g
        slope = jnp.mean(t * unit, axis=-1, keepdims=True)
        out[f] = jnp.where(f < length, scale * (t - unit * slope), 0.0)


def call(kernel, outs, ins, scratch=(), flops=0, limit=40):
    return pl.pallas_call(
        kernel,
        out_shape=outs,
        in_specs=ins,
        out_specs=jax.tree.map(lambda _: VM, outs),
        scratch_shapes=list(scratch),
        compiler_params=pltpu.CompilerParams(vmem_limit_bytes=limit * 2**20),
        cost_estimate=pl.CostEstimate(flops=flops, bytes_accessed=1000000, transcendentals=0),
    )


def up_taps(up_weight):
    u = up_weight.astype(F32)
    rows = [u[1] + u[2], u[0], u[0] + u[1], u[2]]
    taps = [
        jnp.concatenate([r[1] + r[2], r[0] + r[1], r[0], r[2]], axis=-1).astype(BF) for r in rows
    ]
    return jnp.stack(taps, 0)


def ring(value, axis, steps):
    count = lax.axis_size(axis)
    return lax.ppermute(value, axis, [(i, (i + steps) % count) for i in range(count)])


def per_device(latents, counts, norm_gain, conv_weight, up_weight, pixel_grad):
    sizes = (lax.axis_size("section"), lax.axis_size("tile"))
    lat, pg = latents[:, 0], pixel_grad[:, 0]
    gain = norm_gain.reshape(1, C)
    sd = jax.ShapeDtypeStruct
    kern = lambda k: functools.partial(k, sizes)
    wide = conv_weight.reshape(3, 3, 3 * C, C)

    def strip(a, b):
        return jnp.concatenate([lat[:, :, a:b], pg[:, :, a:b]], 1)

    from_left = ring(strip(BW - 2, BW), "tile", 1)
    from_right = ring(strip(0, 2), "tile", -1)
    upw = up_taps(up_weight)
    halo = jnp.concatenate(
        [from_right, jnp.zeros((F, 3 * BR, 4, C), BF), from_left], 2
    )
    own = call(kern(acts_kernel), sd((F, BR, CP, C), BF), [VM, VM, VM])(lat, halo, gain)
    above = ring(own[:, 2:4], "tile", GCOL)
    below = ring(own[:, 0:2], "tile", -GCOL)
    gh = call(
        kern(grad_hidden_kernel),
        sd((F, 6, CP, C), BF),
        [SM, VM, VM, VM],
        [pltpu.VMEM((2, F, BR * CP, 2 * C), BF), pltpu.VMEM((F, 6 * CP, C), F32)],
        flops=3 * 10**9,
    )(counts, pg, halo, upw)
    acc, early = call(
        back_kernel,
        (sd((F, 8 * BW, C), F32), sd((2, 8 * BW, C), BF)),
        [VM, ANY],
        [
            pltpu.VMEM((3, 3 * C, 3 * C), BF),
            pltpu.VMEM((F, 6 * BW, 3 * C), BF),
            pltpu.VMEM((F + 2, 8 * BW, C), F32),
            pltpu.SemaphoreType.DMA((27,)),
        ],
        flops=6 * 10**9,
    )(gh, conv_weight)
    edge = call(kern(edge_frames_kernel), sd((2, 8, CP, C), BF), [SM, VM, VM, VM])(
        counts, own, above, below
    )
    prior = ring(edge, "section", 1)
    later = ring(early, "section", -1)
    part = call(
        kern(forward_kernel),
        sd((F, 6 * CP, C), F32),
        [VM, VM, VM, ANY],
        [
            pltpu.VMEM((9, 3 * C, C), BF),
            pltpu.VMEM((F, 8 * CP, 3 * C), BF),
            pltpu.SemaphoreType.DMA((9,)),
        ],
        flops=6 * 10**9,
    )(own, above, below, wide)
    top, bottom, mine = call(
        kern(later_group_kernel),
        (sd((F, 2 * BW, C), BF), sd((F, 2 * BW, C), BF), sd((F, 4 * BW, C), F32)),
        [SM, VM, VM],
        [pltpu.VMEM((F, 8 * BW, C), F32)],
    )(counts, acc, later)
    from_above = ring(bottom, "tile", GCOL)
    from_below = ring(top, "tile", -GCOL)
    decoded = call(
        kern(decode_kernel),
        sd((F, 2 * BR, BW, C), BF),
        [SM, VM, VM, ANY, VM],
        [
            pltpu.VMEM((6, 3 * C, C), BF),
            pltpu.VMEM((2, 8 * CP, 3 * C), BF),
            pltpu.VMEM((2, F, 4 * CP, 2 * C), BF),
            pltpu.SemaphoreType.DMA((6,)),
        ],
        flops=4 * 10**9,
    )(counts, part, prior, wide, upw)
    grad = call(
        kern(latent_grad_kernel), sd((F, BR, BW, C), F32), [SM, VM, VM, VM, VM, VM]
    )(counts, lat, gain, mine, from_above, from_below)
    return (decoded[:, None], grad[:, None])


def solution(mesh):
    blocks = P("section", "tile", None, None, None)
    return jax.shard_map(
        per_device,
        mesh=mesh,
        in_specs=(blocks, P(), P(), P(), P(), blocks),
        out_specs=(blocks, blocks),
        check_vma=False,
    )
```

profile of v0, /device:TPU:6, one launch (start us, length us, event | category | flops | bytes accessed | tf_op | source)
XLA Modules:
  0.0 69.5 jit_solution(2649506564733042592)
XLA Ops:
  0.6 1.0 %fusion.18 = (bf16[4,4,2,384]{3,2,1,0:T(2,128)(2,1)S(1)}, bf16[4,4,2,384]{3,2,1,0:T(2,128)(2,1)S(1)}) fusion(bf16[4,4,24,384]{3,2,1,0:T(8,128)(2,1)} %bitcast.41), kind=kLoop, calls=%fused_computation.40 | loop fusion | bytes 98304 | tf_op jit(solution)/shard_map/slice | solution.py:298
  1.6 1.1 %fusion.16 = (bf16[4,8,2,384]{3,2,1,0:T(2,128)(2,1)S(1)}, bf16[4,8,2,384]{3,2,1,0:T(2,128)(2,1)S(1)}) fusion(bf16[4,8,24,384]{3,2,1,0:T(8,128)(2,1)} %bitcast.44), kind=kLoop, calls=%fused_computation.38 | loop fusion | bytes 196608 | tf_op jit(solution)/shard_map/slice | solution.py:298
  2.7 0.1 pad_maximum_fusion.1
  2.8 7.8 %collective-permute-start = (bf16[4,12,2,384]{3,2,1,0:T(2,128)(2,1)S(1)}, bf16[4,12,2,384]{3,2,1,0:T(2,128)(2,1)S(1)}, u32[]{:S(2)}, u32[]{:S(2)}) collective-permute-start(bf16[4,12,2,384]{3,2,1,0:T(2,128)(2,1)S(1)} %pad_maximum_fusion.1), channel_id=1, source_target_pairs={{0,63},{1,0},{2,1},{3,2},{4,3},{5,4},{6,5},{7,6},{8,7},{9,8},{10,9... | collective-permute-start | bytes 221192 | tf_op jit(solution)/shard_map/ppermute | solution.py:286
  10.7 0.1 pad_maximum_fusion.2
  10.8 0.1 collective-permute-start.1
  10.8 2.5 %copy.8 = bf16[3,3,384,192]{3,2,1,0:T(8,128)(2,1)S(1)} copy(bf16[3,3,384,192]{2,3,1,0:T(8,128)(2,1)} %param.10) | data formatting | bytes 2654208 | tf_op args[4]
  13.4 0.3 convert_element_type.35
  13.7 0.3 slice_add_fusion.1
  14.1 0.2 fusion.12
  14.3 0.1 fusion.1
  14.3 0.2 fusion.8
  14.5 0.0 copy-start.3
  14.6 0.0 copy-start.1
  14.6 0.0 copy-start.2
  14.6 0.1 fusion.3
  14.7 0.0 slice-start
  14.7 3.6 %maximum_maximum_fusion.upw = bf16[4,384,768]{2,1,0:T(8,128)(2,1)S(1)} fusion(bf16[1,384,192]{2,1,0:T(8,128)(2,1)S(1)} %get-tuple-element.22, bf16[1,384,192]{2,1,0:T(8,128)(2,1)S(1)} %get-tuple-element.21, bf16[1,384,192]{2,1,0:T(8,128)(2,1)S(1)} %get-tuple-element.19, bf16[1,384,192]{2,1,0:T(8,128)(2,1)S(1)} %get-tuple-element.17, ...), kind=kLoop, calls=%fused_computation | loop fusion | flops 37748736 | bytes 4718592 | tf_op jit(solution)/shard_map/stack | solution.py:281
  18.3 0.0 copy-done.3
  18.3 0.1 pad.17.clone
  18.4 0.0 collective-permute-done
  18.4 0.0 collective-permute-done.1
  18.4 0.2 pad_maximum_fusion.halo
  18.6 0.0 copy-done.1
  18.6 0.0 copy-done.2
  18.6 0.0 slice-start.1
  18.7 2.4 %shard_map.81.gh = bf16[4,6,32,384]{3,2,1,0:T(8,128)(2,1)S(1)} custom-call(s32[4]{0:T(128)S(1)} %copy-done.2, bf16[4,8,24,384]{3,2,1,0:T(8,128)(2,1)S(1)} %bitcast.45, bf16[4,12,8,384]{3,2,1,0:T(8,128)(2,1)S(1)} %pad_maximum_fusion.halo, bf16[4,384,768]{2,1,0:T(8,128)(2,1)S(1)} %maximum_maximum_fusion.upw), custom_call_target="tpu_custom_call" | custom-call | flops 3000000000 | bytes 1000000 | tf_op jit(solution)/shard_map/pallas_call | solution.py:309
  21.0 0.0 slice-done
  21.1 0.0 copy-start
  21.1 8.6 %shard_map.82 = (f32[4,192,384]{2,1,0:T(8,128)S(1)}, bf16[2,192,384]{2,1,0:T(8,128)(2,1)S(1)}) custom-call(bf16[4,6,32,384]{3,2,1,0:T(8,128)(2,1)S(1)} %shard_map.81.gh, bf16[3,3,3,384,384]{4,3,2,1,0:T(8,128)(2,1)S(1)} %bitcast.47), custom_call_target="tpu_custom_call" | custom-call | flops 6000000000 | bytes 1000000 | tf_op jit(solution)/shard_map/pallas_call | solution.py:316
  29.7 1.1 %collective-permute-start.5 = (bf16[2,192,384]{2,1,0:T(8,128)(2,1)S(1)}, bf16[2,192,384]{2,1,0:T(8,128)(2,1)S(1)}, u32[]{:S(2)}, u32[]{:S(2)}) collective-permute-start(bf16[2,192,384]{2,1,0:T(8,128)(2,1)S(1)} %get-tuple-element.8), channel_id=1, source_target_pairs={{0,192},{64,0},{128,64},{192,128},{1,193},{65,1},{129,65},{193,129... | collective-permute-start | bytes 884744 | tf_op jit(solution)/shard_map/ppermute | solution.py:286
  30.8 0.3 shard_map.77.own
  31.1 0.1 collective-permute-start.2
  31.2 5.6 %collective-permute-start.3 = (bf16[4,2,32,384]{3,2,1,0:T(8,128)(2,1)S(1)}, bf16[4,2,32,384]{3,2,1,0:T(8,128)(2,1)S(1)}, u32[]{:S(2)}, u32[]{:S(2)}) collective-permute-start(bf16[4,2,32,384]{3,2,1,0:T(8,128)(2,1)S(1)} %get-tuple-element.34), channel_id=1, source_target_pairs={{0,60},{1,61},{2,62},{3,63},{4,0},{5,1},{6,2},{7,3},{8,4},{9,5},{1... | collective-permute-start | bytes 589832 | tf_op jit(solution)/shard_map/ppermute | solution.py:286
  36.8 3.7 %collective-permute-done.2.above = bf16[4,2,32,384]{3,2,1,0:T(8,128)(2,1)S(1)} collective-permute-done((bf16[4,2,32,384]{3,2,1,0:T(8,128)(2,1)S(1)}, bf16[4,2,32,384]{3,2,1,0:T(8,128)(2,1)S(1)}, u32[]{:S(2)}, u32[]{:S(2)}) %collective-permute-start.2) | collective-permute-done | bytes 196640 | tf_op jit(solution)/shard_map/ppermute | solution.py:286
  40.5 0.0 collective-permute-done.3.below
  40.5 0.6 shard_map.79
  41.2 2.5 %collective-permute-start.4 = (bf16[2,8,32,384]{3,2,1,0:T(8,128)(2,1)S(1)}, bf16[2,8,32,384]{3,2,1,0:T(8,128)(2,1)S(1)}, u32[]{:S(2)}, u32[]{:S(2)}) collective-permute-start(bf16[2,8,32,384]{3,2,1,0:T(8,128)(2,1)S(1)} %shard_map.79), channel_id=1, source_target_pairs={{0,64},{64,128},{128,192},{192,0},{1,65},{65,129},{129,193},{193,1... | collective-permute-start | bytes 1179656 | tf_op jit(solution)/shard_map/ppermute | solution.py:286
  43.6 0.0 collective-permute-done.5.later
  43.6 0.8 %shard_map.83 = (bf16[4,48,384]{2,1,0:T(8,128)(2,1)S(1)}, bf16[4,48,384]{2,1,0:T(8,128)(2,1)S(1)}, f32[4,96,384]{2,1,0:T(8,128)S(1)}) custom-call(s32[4]{0:T(128)S(1)} %copy-done.2, f32[4,192,384]{2,1,0:T(8,128)S(1)} %get-tuple-element.7.acc, bf16[2,192,384]{2,1,0:T(8,128)(2,1)S(1)} %collective-permute-done.5.later), custom_call_target="tpu_custom_call" | custom-call | bytes 1000000 | tf_op jit(solution)/shard_map/pallas_call | solution.py:344
  44.4 0.3 collective-permute-start.6
  44.7 5.6 %collective-permute-start.7 = (bf16[4,48,384]{2,1,0:T(8,128)(2,1)S(1)}, bf16[4,48,384]{2,1,0:T(8,128)(2,1)S(1)}, u32[]{:S(2)}, u32[]{:S(2)}) collective-permute-start(bf16[4,48,384]{2,1,0:T(8,128)(2,1)S(1)} %get-tuple-element.11), channel_id=1, source_target_pairs={{0,60},{1,61},{2,62},{3,63},{4,0},{5,1},{6,2},{7,3},{8,4},{9,5},{1... | collective-permute-start | bytes 442376 | tf_op jit(solution)/shard_map/ppermute | solution.py:286
  50.3 10.2 %shard_map.78.part = f32[4,192,384]{2,1,0:T(8,128)S(1)} custom-call(bf16[4,4,32,384]{3,2,1,0:T(8,128)(2,1)S(1)} %shard_map.77.own, bf16[4,2,32,384]{3,2,1,0:T(8,128)(2,1)S(1)} %collective-permute-done.2.above, bf16[4,2,32,384]{3,2,1,0:T(8,128)(2,1)S(1)} %collective-permute-done.3.below, bf16[3,3,1152,384]{3,2,1,0:T(8,128)(2,1)S(1)} %bitcast.48), custom_call_target="tpu_custom_call" | custom-call | flops 6000000000 | bytes 1000000 | tf_op jit(solution)/shard_map/pallas_call | solution.py:333
  60.6 0.0 collective-permute-done.6.above
  60.6 0.0 collective-permute-done.7.below
  60.6 1.8 %shard_map.84 = f32[4,4,24,384]{3,2,1,0:T(8,128)} custom-call(s32[4]{0:T(128)S(1)} %copy-done.2, bf16[4,4,24,384]{3,2,1,0:T(8,128)(2,1)S(1)} %bitcast.43, f32[1,384]{1,0:T(1,128)S(1)} %reshape.274.gain, f32[4,96,384]{2,1,0:T(8,128)S(1)} %get-tuple-element.9.own, bf16[4,48,384]{2,1,0:T(8,128)(2,1)S(1)} %collective-permute-done.6.above, ...), custom_call_target="tpu_custom_call" | custom-call | bytes 1000000 | tf_op jit(solution)/shard_map/pallas_call | solution.py:364
  62.4 0.0 collective-permute-done.4.prior
  62.4 6.9 %shard_map.80 = bf16[4,8,24,384]{3,2,1,0:T(8,128)(2,1)} custom-call(s32[4]{0:T(128)S(1)} %copy-done.2, f32[4,192,384]{2,1,0:T(8,128)S(1)} %shard_map.78.part, bf16[2,8,32,384]{3,2,1,0:T(8,128)(2,1)S(1)} %collective-permute-done.4.prior, bf16[3,3,1152,384]{3,2,1,0:T(8,128)(2,1)S(1)} %bitcast.49, bf16[4,384,768]{2,1,0:T(8,128)(2,1)S(1)} %maximum_maximum_fusion.upw), custom_call_target="tpu_custom_call" | custom-call | flops 4000000000 | bytes 1000000 | tf_op jit(solution)/shard_map/pallas_call | solution.py:352
  (6 shorter events, 0.1 us)
Async XLA Ops:
  2.8 15.6 %collective-permute-start = (bf16[4,12,2,384]{3,2,1,0:T(2,128)(2,1)S(1)}, bf16[4,12,2,384]{3,2,1,0:T(2,128)(2,1)S(1)}, u32[]{:S(2)}, u32[]{:S(2)}) collective-permute-start(bf16[4,12,2,384]{3,2,1,0:T(2,128)(2,1)S(1)} %pad_maximum_fusion.1), channel_id=1, source_target_pairs={{0,63},{1,0},{2,1},{3,2},{4,3},{5,4},{6,5},{7,6},{8,7},{9,8},{10,9... | collective-permute-start | bytes 221192 | tf_op jit(solution)/shard_map/ppermute | solution.py:286
  10.8 7.7 %collective-permute-start.1 = (bf16[4,12,2,384]{3,2,1,0:T(2,128)(2,1)S(1)}, bf16[4,12,2,384]{3,2,1,0:T(2,128)(2,1)S(1)}, u32[]{:S(2)}, u32[]{:S(2)}) collective-permute-start(bf16[4,12,2,384]{3,2,1,0:T(2,128)(2,1)S(1)} %pad_maximum_fusion.2), channel_id=1, source_target_pairs={{0,1},{1,2},{2,3},{3,4},{4,5},{5,6},{6,7},{7,8},{8,9},{9,10},{10,1... | collective-permute-start | bytes 221192 | tf_op jit(solution)/shard_map/ppermute | solution.py:286
  14.5 3.8 %copy-start.3 = (f32[384]{0:T(512)S(1)}, f32[384]{0:T(512)}, u32[]{:S(2)}) copy-start(f32[384]{0:T(512)} %param.8) | copy-start | bytes 4612
  14.6 4.1 %copy-start.1 = (bf16[4,1,8,24,384]{4,3,2,1,0:T(8,128)(2,1)S(1)}, bf16[4,1,8,24,384]{4,3,2,1,0:T(8,128)(2,1)}, u32[]{:S(2)}) copy-start(bf16[4,1,8,24,384]{4,3,2,1,0:T(8,128)(2,1)} %param.11) | copy-start | bytes 1769476
  14.6 4.1 %copy-start.2 = (s32[4]{0:T(128)S(1)}, s32[4]{0:T(128)}, u32[]{:S(2)}) copy-start(s32[4]{0:T(128)} %counts.9) | copy-start | bytes 52
  14.7 6.4 %slice-start = ((s8[7962624]{0:T(1024)(128)(4,1)}), s8[4194304]{0:T(1024)(128)(4,1)S(1)}, s32[]{:S(2)}) async-start(s8[7962624]{0:T(1024)(128)(4,1)} %bitcast.46), calls=%async_computation | async-start | bytes 8388608
  18.6 2.4 %slice-start.1 = ((s8[7962624]{0:T(1024)(128)(4,1)}), s8[3768320]{0:T(1024)(128)(4,1)S(1)}, s32[]{:S(2)}) async-start(s8[7962624]{0:T(1024)(128)(4,1)} %bitcast.46), calls=%async_computation.1 | async-start | bytes 7536640
  21.1 9.7 %copy-start = (bf16[4,1,4,24,384]{4,3,2,1,0:T(8,128)(2,1)S(1)}, bf16[4,1,4,24,384]{4,3,2,1,0:T(8,128)(2,1)}, u32[]{:S(2)}) copy-start(bf16[4,1,4,24,384]{4,3,2,1,0:T(8,128)(2,1)} %param.6) | copy-start | bytes 884740
  29.7 14.0 %collective-permute-start.5 = (bf16[2,192,384]{2,1,0:T(8,128)(2,1)S(1)}, bf16[2,192,384]{2,1,0:T(8,128)(2,1)S(1)}, u32[]{:S(2)}, u32[]{:S(2)}) collective-permute-start(bf16[2,192,384]{2,1,0:T(8,128)(2,1)S(1)} %get-tuple-element.8), channel_id=1, source_target_pairs={{0,192},{64,0},{128,64},{192,128},{1,193},{65,1},{129,65},{193,129... | collective-permute-start | bytes 884744 | tf_op jit(solution)/shard_map/ppermute | solution.py:286
  31.1 9.5 %collective-permute-start.2 = (bf16[4,2,32,384]{3,2,1,0:T(8,128)(2,1)S(1)}, bf16[4,2,32,384]{3,2,1,0:T(8,128)(2,1)S(1)}, u32[]{:S(2)}, u32[]{:S(2)}) collective-permute-start(bf16[4,2,32,384]{3,2,1,0:T(8,128)(2,1)S(1)} %get-tuple-element.35), channel_id=1, source_target_pairs={{0,4},{1,5},{2,6},{3,7},{4,8},{5,9},{6,10},{7,11},{8,12},{9,13},{1... | collective-permute-start | bytes 589832 | tf_op jit(solution)/shard_map/ppermute | solution.py:286
  31.2 9.4 %collective-permute-start.3 = (bf16[4,2,32,384]{3,2,1,0:T(8,128)(2,1)S(1)}, bf16[4,2,32,384]{3,2,1,0:T(8,128)(2,1)S(1)}, u32[]{:S(2)}, u32[]{:S(2)}) collective-permute-start(bf16[4,2,32,384]{3,2,1,0:T(8,128)(2,1)S(1)} %get-tuple-element.34), channel_id=1, source_target_pairs={{0,60},{1,61},{2,62},{3,63},{4,0},{5,1},{6,2},{7,3},{8,4},{9,5},{1... | collective-permute-start | bytes 589832 | tf_op jit(solution)/shard_map/ppermute | solution.py:286
  41.2 21.3 %collective-permute-start.4 = (bf16[2,8,32,384]{3,2,1,0:T(8,128)(2,1)S(1)}, bf16[2,8,32,384]{3,2,1,0:T(8,128)(2,1)S(1)}, u32[]{:S(2)}, u32[]{:S(2)}) collective-permute-start(bf16[2,8,32,384]{3,2,1,0:T(8,128)(2,1)S(1)} %shard_map.79), channel_id=1, source_target_pairs={{0,64},{64,128},{128,192},{192,0},{1,65},{65,129},{129,193},{193,1... | collective-permute-start | bytes 1179656 | tf_op jit(solution)/shard_map/ppermute | solution.py:286
  44.4 16.2 %collective-permute-start.6 = (bf16[4,48,384]{2,1,0:T(8,128)(2,1)S(1)}, bf16[4,48,384]{2,1,0:T(8,128)(2,1)S(1)}, u32[]{:S(2)}, u32[]{:S(2)}) collective-permute-start(bf16[4,48,384]{2,1,0:T(8,128)(2,1)S(1)} %get-tuple-element.10), channel_id=1, source_target_pairs={{0,4},{1,5},{2,6},{3,7},{4,8},{5,9},{6,10},{7,11},{8,12},{9,13},{1... | collective-permute-start | bytes 442376 | tf_op jit(solution)/shard_map/ppermute | solution.py:286
  44.7 15.9 %collective-permute-start.7 = (bf16[4,48,384]{2,1,0:T(8,128)(2,1)S(1)}, bf16[4,48,384]{2,1,0:T(8,128)(2,1)S(1)}, u32[]{:S(2)}, u32[]{:S(2)}) collective-permute-start(bf16[4,48,384]{2,1,0:T(8,128)(2,1)S(1)} %get-tuple-element.11), channel_id=1, source_target_pairs={{0,60},{1,61},{2,62},{3,63},{4,0},{5,1},{6,2},{7,3},{8,4},{9,5},{1... | collective-permute-start | bytes 442376 | tf_op jit(solution)/shard_map/ppermute | solution.py:286
where the time goes:
time: 69.7 us; the launch traced here: 69.5 us
  Pallas kernels  31.5 us (45%)
  starting transfers between devices  23.1 us (33%)
  other arithmetic  5.07 us (7%)
  local copies, waits for them, and re-layouts  4.94 us (7%)
  waiting for transfers between devices  3.75 us (5%)
  between operations  1.09 us (2%)
    ppermute x8, starting transfers between devices, ring(): lax.ppermute(value, axis, [(i, (i + steps) % count) for i in range(count)])  23.1 us
    pallas_call x1, Pallas kernels, per_device(): call(kern(forward_kernel), sd((F, 6 * CP, C), F32), [VM, VM, VM, ANY], [p...  10.2 us
    pallas_call x1, Pallas kernels, per_device(): call(back_kernel, (sd((F, 8 * BW, C), F32), sd((2, 8 * BW, C), BF)), [VM,...  8.59 us
    pallas_call x1, Pallas kernels, per_device(): call(kern(decode_kernel), sd((F, 2 * BR, BW, C), BF), [SM, VM, VM, ANY, V...  6.85 us
    ppermute x8, waiting for transfers between devices, ring(): lax.ppermute(value, axis, [(i, (i + steps) % count) for i in range(count)])  3.75 us
    another operation x1, other arithmetic, up_taps(): return jnp.stack(taps, 0)  3.62 us
    unnamed x13, local copies, waits for them, and re-layouts  2.56 us
    pallas_call x1, Pallas kernels, per_device(): call(kern(grad_hidden_kernel), sd((F, 6, CP, C), BF), [SM, VM, VM, VM], [...  2.38 us
  transfers between devices with their start and end apart: 8, of which 1 were waited for; matrix products, arithmetic and copies ran while one was open for 11% of the time, Pallas kernels for 20%

commit v1 on v0

--- a/solution.py
+++ b/solution.py
@@ -62,8 +62,20 @@
         out[f] = jnp.where(mask, activate(whole, g), 0.0).astype(BF)
 
 
-def grad_hidden_kernel(sizes, counts, pg, halo, upw, out, parts, acc):
-    where = place_of(sizes)
+def up_taps(up, upw):
+    rows = (((1, 2), (0,)), ((0, 1), (2,)))
+    columns = ((1, 2), (0, 1), (0,), (2,))
+    for k in range(2):
+        for a in range(2):
+            sums = [sum(up[dr, dc].astype(F32) for dr in rows[k][a]) for dc in range(3)]
+            for b in range(4):
+                total = sum(sums[dc] for dc in columns[b])
+                upw[k, b * (C // 2) : (b + 1) * (C // 2), a * C : (a + 1) * C] = total.astype(BF)
+
+
+def grad_hidden_kernel(sizes, counts, pg, halo, up, own, out, upw, parts, acc):
+    where = place_of(sizes)
+    up_taps(up, upw)
     length = counts[where["section"]]
     mask = column_mask(where, C, 2)
     low = lax.broadcasted_iota(jnp.int32, (1, CP, C), 2) < C // 2
@@ -81,14 +93,15 @@
     even = parts[0].reshape(F * BR * CP, 2 * C)
     odd = parts[1].reshape(F * BR * CP, 2 * C)
 
-    def term(x, w):
-        return lax.dot_general(x, upw[w], NT, preferred_element_type=F32).reshape(F, BR * CP, C)
-
-    acc[:, CP : 5 * CP] = term(even, 0) + term(odd, 2)
+    def term(x, k, a):
+        taps = upw[k, :, a * C : (a + 1) * C]
+        return jnp.dot(x, taps, preferred_element_type=F32).reshape(F, BR * CP, C)
+
+    acc[:, CP : 5 * CP] = term(even, 0, 0) + term(odd, 1, 0)
     acc[:, 0:CP] = jnp.zeros((F, CP, C), F32)
     acc[:, 5 * CP : 6 * CP] = jnp.zeros((F, CP, C), F32)
-    acc[:, 0 : 4 * CP] += term(even, 1)
-    acc[:, 2 * CP : 6 * CP] += term(odd, 3)
+    acc[:, 0 : 4 * CP] += term(even, 0, 1)
+    acc[:, 2 * CP : 6 * CP] += term(odd, 1, 1)
     inner = column_mask(where, C, 1)
     for f in range(F):
         value = acc[f].reshape(6, CP, C)
@@ -130,7 +143,8 @@
     acc_out[...] = acc[2:6]
 
 
-def edge_frames_kernel(sizes, counts, own, above, below, out):
+def edge_frames_kernel(sizes, counts, own, above, below, early, out, early_out):
+    early_out[...] = early[...]
     where = place_of(sizes)
     length = counts[where["section"]]
     for k in range(2):
@@ -216,10 +230,8 @@
         pairs[1, f, :, C : 2 * C] = hidden[2 * CP : 6 * CP]
     low = lax.broadcasted_iota(jnp.int32, (1, CP, C), 2) < C // 2
     for k in range(2):
-        rows = jnp.dot(
-            pairs[k].reshape(F * 4 * CP, 2 * C),
-            upw[2 * k : 2 * k + 2].reshape(2 * C, 2 * C),
-            preferred_element_type=F32,
+        rows = lax.dot_general(
+            pairs[k].reshape(F * 4 * CP, 2 * C), upw[k], NT, preferred_element_type=F32
         )
         for f in range(F):
             whole = rows[f * 4 * CP : (f + 1) * 4 * CP].reshape(4, CP, 2 * C)
@@ -272,15 +284,6 @@
     )
 
 
-def up_taps(up_weight):
-    u = up_weight.astype(F32)
-    rows = [u[1] + u[2], u[0], u[0] + u[1], u[2]]
-    taps = [
-        jnp.concatenate([r[1] + r[2], r[0] + r[1], r[0], r[2]], axis=-1).astype(BF) for r in rows
-    ]
-    return jnp.stack(taps, 0)
-
-
 def ring(value, axis, steps):
     count = lax.axis_size(axis)
     return lax.ppermute(value, axis, [(i, (i + steps) % count) for i in range(count)])
@@ -299,20 +302,19 @@
 
     from_left = ring(strip(BW - 2, BW), "tile", 1)
     from_right = ring(strip(0, 2), "tile", -1)
-    upw = up_taps(up_weight)
     halo = jnp.concatenate(
         [from_right, jnp.zeros((F, 3 * BR, 4, C), BF), from_left], 2
     )
     own = call(kern(acts_kernel), sd((F, BR, CP, C), BF), [VM, VM, VM])(lat, halo, gain)
     above = ring(own[:, 2:4], "tile", GCOL)
     below = ring(own[:, 0:2], "tile", -GCOL)
-    gh = call(
+    gh, upw = call(
         kern(grad_hidden_kernel),
-        sd((F, 6, CP, C), BF),
-        [SM, VM, VM, VM],
+        (sd((F, 6, CP, C), BF), sd((2, 2 * C, 2 * C), BF)),
+        [SM, VM, VM, VM, ANY],
         [pltpu.VMEM((2, F, BR * CP, 2 * C), BF), pltpu.VMEM((F, 6 * CP, C), F32)],
         flops=3 * 10**9,
-    )(counts, pg, halo, upw)
+    )(counts, pg, halo, jnp.transpose(up_weight, (0, 1, 3, 2)), own)
     acc, early = call(
         back_kernel,
         (sd((F, 8 * BW, C), F32), sd((2, 8 * BW, C), BF)),
@@ -325,9 +327,11 @@
         ],
         flops=6 * 10**9,
     )(gh, conv_weight)
-    edge = call(kern(edge_frames_kernel), sd((2, 8, CP, C), BF), [SM, VM, VM, VM])(
-        counts, own, above, below
-    )
+    edge, early = call(
+        kern(edge_frames_kernel),
+        (sd((2, 8, CP, C), BF), sd((2, 8 * BW, C), BF)),
+        [SM, VM, VM, VM, VM],
+    )(counts, own, above, below, early)
     prior = ring(edge, "section", 1)
     later = ring(early, "section", -1)
     part = call(

time: 69.7 us -> 66.8 us (0.958)
  other arithmetic: 5.07 us -> 0.39 us
  waiting for transfers between devices: 3.75 us -> 6.4 us
    another operation x2 -> x0, other arithmetic: 3.81 us -> none  [the longest x1 3.62 us: up_taps(): return jnp.stack(taps, 0)]
    ppermute x8, waiting for transfers between devices: 3.75 us -> 6.4 us  [ring(): lax.ppermute(value, axis, [(i, (i + steps) % count) for i in range(count)])]
    unnamed x13 -> x12, local copies, waits for them, and re-layouts: 2.56 us -> 1.6 us
  transfers between devices with their start and end apart: 8 -> 8, of which waited for: 1 -> 2; matrix products, arithmetic and copies ran while one was open for 11% -> 1% of each run, Pallas kernels for 20% -> 43%
where the time goes in v1:
time: 66.8 us; the launch traced here: 66.6 us
  Pallas kernels  31.6 us (47%)
  starting transfers between devices  22.8 us (34%)
  waiting for transfers between devices  6.4 us (10%)
  local copies, waits for them, and re-layouts  4.56 us (7%)
  between operations  0.82 us (1%)
    ppermute x8, starting transfers between devices, ring(): lax.ppermute(value, axis, [(i, (i + steps) % count) for i in range(count)])  22.8 us
    pallas_call x1, Pallas kernels, per_device(): call(kern(forward_kernel), sd((F, 6 * CP, C), F32), [VM, VM, VM, ANY], [p...  10.2 us
    pallas_call x1, Pallas kernels, per_device(): call(back_kernel, (sd((F, 8 * BW, C), F32), sd((2, 8 * BW, C), BF)), [VM,...  8.59 us
    pallas_call x1, Pallas kernels, per_device(): call(kern(decode_kernel), sd((F, 2 * BR, BW, C), BF), [SM, VM, VM, ANY, V...  6.69 us
    ppermute x8, waiting for transfers between devices, ring(): lax.ppermute(value, axis, [(i, (i + steps) % count) for i in range(count)])  6.4 us
    pallas_call x1, Pallas kernels, per_device(): call(kern(grad_hidden_kernel), (sd((F, 6, CP, C), BF), sd((2, 2 * C, 2 *...  2.62 us
    slice x2, local copies, waits for them, and re-layouts, strip(): return jnp.concatenate([lat[:, :, a:b], pg[:, :, a:b]], 1)  2.15 us
    pallas_call x1, Pallas kernels, per_device(): call(kern(latent_grad_kernel), sd((F, BR, BW, C), F32), [SM, VM, VM, VM,...  1.82 us
  transfers between devices with their start and end apart: 8, of which 2 were waited for; matrix products, arithmetic and copies ran while one was open for 1% of the time, Pallas kernels for 43%

profile of v1, /device:TPU:6, one launch (start us, length us, event | category | flops | bytes accessed | tf_op | source)
XLA Modules:
  0.0 66.6 jit_solution(16188527343353529102)
XLA Ops:
  0.6 1.0 %fusion.2 = (bf16[4,4,2,384]{3,2,1,0:T(2,128)(2,1)S(1)}, bf16[4,4,2,384]{3,2,1,0:T(2,128)(2,1)S(1)}) fusion(bf16[4,4,24,384]{3,2,1,0:T(8,128)(2,1)} %bitcast.10), kind=kLoop, calls=%fused_computation.5 | loop fusion | bytes 98304 | tf_op jit(solution)/shard_map/slice | solution.py:301
  1.6 0.0 copy-start.2
  1.6 0.0 copy-start.3
  1.6 1.2 %fusion = (bf16[4,8,2,384]{3,2,1,0:T(2,128)(2,1)S(1)}, bf16[4,8,2,384]{3,2,1,0:T(2,128)(2,1)S(1)}) fusion(bf16[4,8,24,384]{3,2,1,0:T(8,128)(2,1)} %bitcast.13), kind=kLoop, calls=%fused_computation.3 | loop fusion | bytes 196608 | tf_op jit(solution)/shard_map/slice | solution.py:301
  2.8 0.1 pad_maximum_fusion.1
  2.9 7.8 %collective-permute-start = (bf16[4,12,2,384]{3,2,1,0:T(2,128)(2,1)S(1)}, bf16[4,12,2,384]{3,2,1,0:T(2,128)(2,1)S(1)}, u32[]{:S(2)}, u32[]{:S(2)}) collective-permute-start(bf16[4,12,2,384]{3,2,1,0:T(2,128)(2,1)S(1)} %pad_maximum_fusion.1), channel_id=1, source_target_pairs={{0,63},{1,0},{2,1},{3,2},{4,3},{5,4},{6,5},{7,6},{8,7},{9,8},{10,9... | collective-permute-start | bytes 221192 | tf_op jit(solution)/shard_map/ppermute | solution.py:289
  10.7 0.1 pad_maximum_fusion.2
  10.8 0.1 collective-permute-start.1
  10.9 0.7 %reshape.10.gain = f32[1,384]{1,0:T(1,128)S(1)} reshape(f32[384]{0:T(512)} %param.8) | data formatting | bytes 3072 | tf_op jit(solution)/shard_map/reshape | solution.py:295
  11.6 0.1 pad.1.clone
  11.7 1.0 %collective-permute-done = bf16[4,12,2,384]{3,2,1,0:T(2,128)(2,1)S(1)} collective-permute-done((bf16[4,12,2,384]{3,2,1,0:T(2,128)(2,1)S(1)}, bf16[4,12,2,384]{3,2,1,0:T(2,128)(2,1)S(1)}, u32[]{:S(2)}, u32[]{:S(2)}) %collective-permute-start) | collective-permute-done | bytes 73760 | tf_op jit(solution)/shard_map/ppermute | solution.py:289
  12.7 5.4 %collective-permute-done.1 = bf16[4,12,2,384]{3,2,1,0:T(2,128)(2,1)S(1)} collective-permute-done((bf16[4,12,2,384]{3,2,1,0:T(2,128)(2,1)S(1)}, bf16[4,12,2,384]{3,2,1,0:T(2,128)(2,1)S(1)}, u32[]{:S(2)}, u32[]{:S(2)}) %collective-permute-start.1) | collective-permute-done | bytes 73760 | tf_op jit(solution)/shard_map/ppermute | solution.py:289
  18.1 0.2 pad_maximum_fusion.halo
  18.3 0.0 copy-start
  18.3 1.0 %copy-done = bf16[4,1,4,24,384]{4,3,2,1,0:T(8,128)(2,1)S(1)} copy-done((bf16[4,1,4,24,384]{4,3,2,1,0:T(8,128)(2,1)S(1)}, bf16[4,1,4,24,384]{4,3,2,1,0:T(8,128)(2,1)}, u32[]{:S(2)}) %copy-start) | copy-done | bytes 294936
  19.2 0.0 copy-start.5
  19.3 0.3 shard_map.77.own
  19.6 0.1 collective-permute-start.2
  19.7 5.6 %collective-permute-start.3 = (bf16[4,2,32,384]{3,2,1,0:T(8,128)(2,1)S(1)}, bf16[4,2,32,384]{3,2,1,0:T(8,128)(2,1)S(1)}, u32[]{:S(2)}, u32[]{:S(2)}) collective-permute-start(bf16[4,2,32,384]{3,2,1,0:T(8,128)(2,1)S(1)} %get-tuple-element.24), channel_id=1, source_target_pairs={{0,60},{1,61},{2,62},{3,63},{4,0},{5,1},{6,2},{7,3},{8,4},{9,5},{1... | collective-permute-start | bytes 589832 | tf_op jit(solution)/shard_map/ppermute | solution.py:289
  25.3 0.0 copy-done.2
  25.3 0.0 copy-done.3
  25.3 0.0 copy-done.5
  25.3 0.0 copy-start.4
  25.3 2.6 %shard_map.79 = (bf16[4,6,32,384]{3,2,1,0:T(8,128)(2,1)S(1)}, bf16[2,768,768]{2,1,0:T(8,128)(2,1)S(1)}) custom-call(s32[4]{0:T(128)S(1)} %copy-done.3, bf16[4,8,24,384]{3,2,1,0:T(8,128)(2,1)S(1)} %bitcast.14, bf16[4,12,8,384]{3,2,1,0:T(8,128)(2,1)S(1)} %pad_maximum_fusion.halo, bf16[3,3,192,384]{3,2,1,0:T(8,128)(2,1)S(1)} %bitcast.17, ...), custom_call_target="tpu_custom_call" | custom-call | flops 3000000000 | bytes 1000000 | tf_op jit(solution)/shard_map/pallas_call | solution.py:311
  27.9 0.6 copy-done.4
  28.6 8.6 %shard_map.80 = (f32[4,192,384]{2,1,0:T(8,128)S(1)}, bf16[2,192,384]{2,1,0:T(8,128)(2,1)S(1)}) custom-call(bf16[4,6,32,384]{3,2,1,0:T(8,128)(2,1)S(1)} %get-tuple-element.11.gh, bf16[3,3,3,384,384]{4,3,2,1,0:T(8,128)(2,1)S(1)} %copy-done.4), custom_call_target="tpu_custom_call" | custom-call | flops 6000000000 | bytes 1000000 | tf_op jit(solution)/shard_map/pallas_call | solution.py:318
  37.2 0.0 collective-permute-done.2.above
  37.2 0.0 collective-permute-done.3.below
  37.2 0.6 shard_map.81
  37.8 1.1 %collective-permute-start.5 = (bf16[2,192,384]{2,1,0:T(8,128)(2,1)S(1)}, bf16[2,192,384]{2,1,0:T(8,128)(2,1)S(1)}, u32[]{:S(2)}, u32[]{:S(2)}) collective-permute-start(bf16[2,192,384]{2,1,0:T(8,128)(2,1)S(1)} %get-tuple-element.16), channel_id=1, source_target_pairs={{0,192},{64,0},{128,64},{192,128},{1,193},{65,1},{129,65},{193,129... | collective-permute-start | bytes 884744 | tf_op jit(solution)/shard_map/ppermute | solution.py:289
  38.9 2.4 %collective-permute-start.4 = (bf16[2,8,32,384]{3,2,1,0:T(8,128)(2,1)S(1)}, bf16[2,8,32,384]{3,2,1,0:T(8,128)(2,1)S(1)}, u32[]{:S(2)}, u32[]{:S(2)}) collective-permute-start(bf16[2,8,32,384]{3,2,1,0:T(8,128)(2,1)S(1)} %get-tuple-element.13), channel_id=1, source_target_pairs={{0,64},{64,128},{128,192},{192,0},{1,65},{65,129},{129,193},{193,1... | collective-permute-start | bytes 1179656 | tf_op jit(solution)/shard_map/ppermute | solution.py:289
  41.3 10.2 %shard_map.78.part = f32[4,192,384]{2,1,0:T(8,128)S(1)} custom-call(bf16[4,4,32,384]{3,2,1,0:T(8,128)(2,1)S(1)} %shard_map.77.own, bf16[4,2,32,384]{3,2,1,0:T(8,128)(2,1)S(1)} %collective-permute-done.2.above, bf16[4,2,32,384]{3,2,1,0:T(8,128)(2,1)S(1)} %collective-permute-done.3.below, bf16[3,3,1152,384]{3,2,1,0:T(8,128)(2,1)S(1)} %bitcast.15), custom_call_target="tpu_custom_call" | custom-call | flops 6000000000 | bytes 1000000 | tf_op jit(solution)/shard_map/pallas_call | solution.py:337
  51.6 0.0 collective-permute-done.5.later
  51.6 0.8 %shard_map.83 = (bf16[4,48,384]{2,1,0:T(8,128)(2,1)S(1)}, bf16[4,48,384]{2,1,0:T(8,128)(2,1)S(1)}, f32[4,96,384]{2,1,0:T(8,128)S(1)}) custom-call(s32[4]{0:T(128)S(1)} %copy-done.3, f32[4,192,384]{2,1,0:T(8,128)S(1)} %get-tuple-element.15.acc, bf16[2,192,384]{2,1,0:T(8,128)(2,1)S(1)} %collective-permute-done.5.later), custom_call_target="tpu_custom_call" | custom-call | bytes 1000000 | tf_op jit(solution)/shard_map/pallas_call | solution.py:348
  52.3 0.1 collective-permute-start.6
  52.4 5.6 %collective-permute-start.7 = (bf16[4,48,384]{2,1,0:T(8,128)(2,1)S(1)}, bf16[4,48,384]{2,1,0:T(8,128)(2,1)S(1)}, u32[]{:S(2)}, u32[]{:S(2)}) collective-permute-start(bf16[4,48,384]{2,1,0:T(8,128)(2,1)S(1)} %get-tuple-element.19), channel_id=1, source_target_pairs={{0,60},{1,61},{2,62},{3,63},{4,0},{5,1},{6,2},{7,3},{8,4},{9,5},{1... | collective-permute-start | bytes 442376 | tf_op jit(solution)/shard_map/ppermute | solution.py:289
  58.1 0.0 collective-permute-done.4.prior
  58.1 0.0 copy-start.1
  58.1 6.7 %shard_map.82 = bf16[4,8,24,384]{3,2,1,0:T(8,128)(2,1)} custom-call(s32[4]{0:T(128)S(1)} %copy-done.3, f32[4,192,384]{2,1,0:T(8,128)S(1)} %shard_map.78.part, bf16[2,8,32,384]{3,2,1,0:T(8,128)(2,1)S(1)} %collective-permute-done.4.prior, bf16[3,3,1152,384]{3,2,1,0:T(8,128)(2,1)S(1)} %bitcast.16, bf16[2,768,768]{2,1,0:T(8,128)(2,1)S(1)} %get-tuple-element.14.upw), custom_call_target="tpu_custom_call" | custom-call | flops 4000000000 | bytes 1000000 | tf_op jit(solution)/shard_map/pallas_call | solution.py:356
  64.8 0.0 collective-permute-done.6.above
  64.8 0.0 collective-permute-done.7.below
  64.8 0.0 copy-done.1
  64.8 1.8 %shard_map.84 = f32[4,4,24,384]{3,2,1,0:T(8,128)} custom-call(s32[4]{0:T(128)S(1)} %copy-done.3, bf16[4,4,24,384]{3,2,1,0:T(8,128)(2,1)S(1)} %bitcast.12, f32[1,384]{1,0:T(1,128)S(1)} %reshape.10.gain, f32[4,96,384]{2,1,0:T(8,128)S(1)} %get-tuple-element.17.own, bf16[4,48,384]{2,1,0:T(8,128)(2,1)S(1)} %collective-permute-done.6.above, ...), custom_call_target="tpu_custom_call" | custom-call | bytes 1000000 | tf_op jit(solution)/shard_map/pallas_call | solution.py:368
  (2 shorter events, 0.0 us)
Async XLA Ops:
  1.6 23.7 %copy-start.2 = (bf16[4,1,8,24,384]{4,3,2,1,0:T(8,128)(2,1)S(1)}, bf16[4,1,8,24,384]{4,3,2,1,0:T(8,128)(2,1)}, u32[]{:S(2)}) copy-start(bf16[4,1,8,24,384]{4,3,2,1,0:T(8,128)(2,1)} %param.11) | copy-start | bytes 1769476
  1.6 23.7 %copy-start.3 = (s32[4]{0:T(128)S(1)}, s32[4]{0:T(128)}, u32[]{:S(2)}) copy-start(s32[4]{0:T(128)} %counts.9) | copy-start | bytes 52
  2.9 9.8 %collective-permute-start = (bf16[4,12,2,384]{3,2,1,0:T(2,128)(2,1)S(1)}, bf16[4,12,2,384]{3,2,1,0:T(2,128)(2,1)S(1)}, u32[]{:S(2)}, u32[]{:S(2)}) collective-permute-start(bf16[4,12,2,384]{3,2,1,0:T(2,128)(2,1)S(1)} %pad_maximum_fusion.1), channel_id=1, source_target_pairs={{0,63},{1,0},{2,1},{3,2},{4,3},{5,4},{6,5},{7,6},{8,7},{9,8},{10,9... | collective-permute-start | bytes 221192 | tf_op jit(solution)/shard_map/ppermute | solution.py:289
  10.8 7.2 %collective-permute-start.1 = (bf16[4,12,2,384]{3,2,1,0:T(2,128)(2,1)S(1)}, bf16[4,12,2,384]{3,2,1,0:T(2,128)(2,1)S(1)}, u32[]{:S(2)}, u32[]{:S(2)}) collective-permute-start(bf16[4,12,2,384]{3,2,1,0:T(2,128)(2,1)S(1)} %pad_maximum_fusion.2), channel_id=1, source_target_pairs={{0,1},{1,2},{2,3},{3,4},{4,5},{5,6},{6,7},{7,8},{8,9},{9,10},{10,1... | collective-permute-start | bytes 221192 | tf_op jit(solution)/shard_map/ppermute | solution.py:289
  18.3 1.0 %copy-start = (bf16[4,1,4,24,384]{4,3,2,1,0:T(8,128)(2,1)S(1)}, bf16[4,1,4,24,384]{4,3,2,1,0:T(8,128)(2,1)}, u32[]{:S(2)}) copy-start(bf16[4,1,4,24,384]{4,3,2,1,0:T(8,128)(2,1)} %param.6) | copy-start | bytes 884740
  19.2 6.0 %copy-start.5 = (bf16[3,3,384,192]{2,3,1,0:T(8,128)(2,1)S(1)}, bf16[3,3,384,192]{2,3,1,0:T(8,128)(2,1)}, u32[]{:S(2)}) copy-start(bf16[3,3,384,192]{2,3,1,0:T(8,128)(2,1)} %param.10) | copy-start | bytes 3981316
  19.6 17.6 %collective-permute-start.2 = (bf16[4,2,32,384]{3,2,1,0:T(8,128)(2,1)S(1)}, bf16[4,2,32,384]{3,2,1,0:T(8,128)(2,1)S(1)}, u32[]{:S(2)}, u32[]{:S(2)}) collective-permute-start(bf16[4,2,32,384]{3,2,1,0:T(8,128)(2,1)S(1)} %get-tuple-element.25), channel_id=1, source_target_pairs={{0,4},{1,5},{2,6},{3,7},{4,8},{5,9},{6,10},{7,11},{8,12},{9,13},{1... | collective-permute-start | bytes 589832 | tf_op jit(solution)/shard_map/ppermute | solution.py:289
  19.7 17.5 %collective-permute-start.3 = (bf16[4,2,32,384]{3,2,1,0:T(8,128)(2,1)S(1)}, bf16[4,2,32,384]{3,2,1,0:T(8,128)(2,1)S(1)}, u32[]{:S(2)}, u32[]{:S(2)}) collective-permute-start(bf16[4,2,32,384]{3,2,1,0:T(8,128)(2,1)S(1)} %get-tuple-element.24), channel_id=1, source_target_pairs={{0,60},{1,61},{2,62},{3,63},{4,0},{5,1},{6,2},{7,3},{8,4},{9,5},{1... | collective-permute-start | bytes 589832 | tf_op jit(solution)/shard_map/ppermute | solution.py:289
  25.3 3.3 %copy-start.4 = (bf16[3,3,3,384,384]{4,3,2,1,0:T(8,128)(2,1)S(1)}, bf16[3,3,3,384,384]{4,3,2,1,0:T(8,128)(2,1)}, u32[]{:S(2)}) copy-start(bf16[3,3,3,384,384]{4,3,2,1,0:T(8,128)(2,1)} %weight.1) | copy-start | bytes 23887876
  37.8 13.8 %collective-permute-start.5 = (bf16[2,192,384]{2,1,0:T(8,128)(2,1)S(1)}, bf16[2,192,384]{2,1,0:T(8,128)(2,1)S(1)}, u32[]{:S(2)}, u32[]{:S(2)}) collective-permute-start(bf16[2,192,384]{2,1,0:T(8,128)(2,1)S(1)} %get-tuple-element.16), channel_id=1, source_target_pairs={{0,192},{64,0},{128,64},{192,128},{1,193},{65,1},{129,65},{193,129... | collective-permute-start | bytes 884744 | tf_op jit(solution)/shard_map/ppermute | solution.py:289
  38.9 19.2 %collective-permute-start.4 = (bf16[2,8,32,384]{3,2,1,0:T(8,128)(2,1)S(1)}, bf16[2,8,32,384]{3,2,1,0:T(8,128)(2,1)S(1)}, u32[]{:S(2)}, u32[]{:S(2)}) collective-permute-start(bf16[2,8,32,384]{3,2,1,0:T(8,128)(2,1)S(1)} %get-tuple-element.13), channel_id=1, source_target_pairs={{0,64},{64,128},{128,192},{192,0},{1,65},{65,129},{129,193},{193,1... | collective-permute-start | bytes 1179656 | tf_op jit(solution)/shard_map/ppermute | solution.py:289
  52.3 12.4 %collective-permute-start.6 = (bf16[4,48,384]{2,1,0:T(8,128)(2,1)S(1)}, bf16[4,48,384]{2,1,0:T(8,128)(2,1)S(1)}, u32[]{:S(2)}, u32[]{:S(2)}) collective-permute-start(bf16[4,48,384]{2,1,0:T(8,128)(2,1)S(1)} %get-tuple-element.18), channel_id=1, source_target_pairs={{0,4},{1,5},{2,6},{3,7},{4,8},{5,9},{6,10},{7,11},{8,12},{9,13},{1... | collective-permute-start | bytes 442376 | tf_op jit(solution)/shard_map/ppermute | solution.py:289
  52.4 12.3 %collective-permute-start.7 = (bf16[4,48,384]{2,1,0:T(8,128)(2,1)S(1)}, bf16[4,48,384]{2,1,0:T(8,128)(2,1)S(1)}, u32[]{:S(2)}, u32[]{:S(2)}) collective-permute-start(bf16[4,48,384]{2,1,0:T(8,128)(2,1)S(1)} %get-tuple-element.19), channel_id=1, source_target_pairs={{0,60},{1,61},{2,62},{3,63},{4,0},{5,1},{6,2},{7,3},{8,4},{9,5},{1... | collective-permute-start | bytes 442376 | tf_op jit(solution)/shard_map/ppermute | solution.py:289
  58.1 6.7 %copy-start.1 = (bf16[4,1,4,24,384]{4,3,2,1,0:T(8,128)(2,1)S(1)}, bf16[4,1,4,24,384]{4,3,2,1,0:T(8,128)(2,1)}, u32[]{:S(2)}) copy-start(bf16[4,1,4,24,384]{4,3,2,1,0:T(8,128)(2,1)} %param.6) | copy-start | bytes 884740

commit v2 on v1

--- a/solution.py
+++ b/solution.py
@@ -163,13 +163,7 @@
         ).astype(BF)
 
 
-def forward_kernel(sizes, own, above, below, weight, acc_out, wt, cells, sems):
-    copies = {}
-    for dt in (2, 1, 0):
-        for dr in range(3):
-            copy = pltpu.make_async_copy(weight.at[dt, dr], wt.at[dt * 3 + dr], sems.at[dt * 3 + dr])
-            copy.start()
-            copies[dt, dr] = copy
+def forward_kernel(sizes, own, above, below, weight, acc_out, cells):
     where = place_of(sizes)
     for f in range(F):
         side_by_side(jnp.where(where["up"], above[f].astype(F32), 0.0), 0, cells, f)
@@ -179,9 +173,8 @@
         count = F - (2 - dt)
         total = None
         for dr in range(3):
-            copies[dt, dr].wait()
             left = cells[0:count, dr * CP : (dr + 6) * CP].reshape(count * 6 * CP, 3 * C)
-            term = jnp.dot(left, wt[dt * 3 + dr], preferred_element_type=F32)
+            term = jnp.dot(left, weight[dt, dr], preferred_element_type=F32)
             total = term if total is None else total + term
         total = total.reshape(count, 6 * CP, C)
         if dt == 2:
@@ -190,13 +183,7 @@
             acc_out[2 - dt : F] += total
 
 
-def decode_kernel(sizes, counts, part, prior, weight, upw, out, wt, cells, pairs, sems):
-    copies = {}
-    for dt in (0, 1):
-        for dr in range(3):
-            copy = pltpu.make_async_copy(weight.at[dt, dr], wt.at[dt * 3 + dr], sems.at[dt * 3 + dr])
-            copy.start()
-            copies[dt, dr] = copy
+def decode_kernel(sizes, counts, part, prior, weight, upw, out, cells, pairs):
     where = place_of(sizes)
     length = counts[where["section"]]
     for k in range(2):
@@ -206,15 +193,11 @@
         total = None
         for dr in range(3):
             left = cells[first : first + count, dr * CP : (dr + 6) * CP].reshape(count * 6 * CP, 3 * C)
-            value = jnp.dot(left, wt[dt * 3 + dr], preferred_element_type=F32)
+            value = jnp.dot(left, weight[dt, dr], preferred_element_type=F32)
             total = value if total is None else total + value
         return total.reshape(count, 6 * CP, C)
 
-    for dr in range(3):
-        copies[0, dr].wait()
     early = part[0:2] + term(0, 2, 0)
-    for dr in range(3):
-        copies[1, dr].wait()
     late = term(1, 1, 1)
     inner = column_mask(where, C, 1)
     row = lax.broadcasted_iota(jnp.int32, (6, CP, C), 0)
@@ -289,6 +272,11 @@
     return lax.ppermute(value, axis, [(i, (i + steps) % count) for i in range(count)])
 
 
+def swap(value, tiles, shift):
+    places = [((at + GCOL + 1 + shift) ^ 1) - GCOL - 1 - shift for at in range(tiles)]
+    return lax.ppermute(value, "tile", [(at, to % tiles) for at, to in enumerate(places)])
+
+
 def per_device(latents, counts, norm_gain, conv_weight, up_weight, pixel_grad):
     sizes = (lax.axis_size("section"), lax.axis_size("tile"))
     lat, pg = latents[:, 0], pixel_grad[:, 0]
@@ -297,14 +285,17 @@
     kern = lambda k: functools.partial(k, sizes)
     wide = conv_weight.reshape(3, 3, 3 * C, C)
 
-    def strip(a, b):
-        return jnp.concatenate([lat[:, :, a:b], pg[:, :, a:b]], 1)
-
-    from_left = ring(strip(BW - 2, BW), "tile", 1)
-    from_right = ring(strip(0, 2), "tile", -1)
-    halo = jnp.concatenate(
-        [from_right, jnp.zeros((F, 3 * BR, 4, C), BF), from_left], 2
-    )
+    tiles = sizes[1]
+    even = lax.rem(lax.axis_index("tile") + GCOL + 1, 2) == 0
+
+    def strip(a):
+        return jnp.concatenate([lat[:, :, a : a + 2], pg[:, :, a : a + 2]], 1)
+
+    first, last = strip(0), strip(BW - 2)
+    one = swap(jnp.where(even, last, first), tiles, 0)
+    two = swap(jnp.where(even, first, last), tiles, 1)
+    from_left, from_right = jnp.where(even, two, one), jnp.where(even, one, two)
+    halo = jnp.concatenate([from_right, jnp.zeros((F, 3 * BR, 4, C), BF), from_left], 2)
     own = call(kern(acts_kernel), sd((F, BR, CP, C), BF), [VM, VM, VM])(lat, halo, gain)
     above = ring(own[:, 2:4], "tile", GCOL)
     below = ring(own[:, 0:2], "tile", -GCOL)
@@ -337,12 +328,8 @@
     part = call(
         kern(forward_kernel),
         sd((F, 6 * CP, C), F32),
-        [VM, VM, VM, ANY],
-        [
-            pltpu.VMEM((9, 3 * C, C), BF),
-            pltpu.VMEM((F, 8 * CP, 3 * C), BF),
-            pltpu.SemaphoreType.DMA((9,)),
-        ],
+        [VM, VM, VM, VM],
+        [pltpu.VMEM((F, 8 * CP, 3 * C), BF)],
         flops=6 * 10**9,
     )(own, above, below, wide)
     top, bottom, mine = call(
@@ -356,12 +343,10 @@
     decoded = call(
         kern(decode_kernel),
         sd((F, 2 * BR, BW, C), BF),
-        [SM, VM, VM, ANY, VM],
+        [SM, VM, VM, VM, VM],
         [
-            pltpu.VMEM((6, 3 * C, C), BF),
             pltpu.VMEM((2, 8 * CP, 3 * C), BF),
             pltpu.VMEM((2, F, 4 * CP, 2 * C), BF),
-            pltpu.SemaphoreType.DMA((6,)),
         ],
         flops=4 * 10**9,
     )(counts, part, prior, wide, upw)

time: 66.8 us -> 55.6 us (0.83)
  waiting for transfers between devices: 6.4 us -> 1.29 us
  Pallas kernels: 31.6 us -> 26.7 us
  local copies, waits for them, and re-layouts: 4.56 us -> 3.59 us
    ppermute x8 -> x6, starting transfers between devices: 22.8 us -> 14.7 us  [ring(): lax.ppermute(value, axis, [(i, (i + steps) % count) for i in range(count)])]
    ppermute x0 -> x2, starting transfers between devices: none -> 7.84 us  [swap(): lax.ppermute(value, 'tile', [(at, to % tiles) for at, to in enumerate(pla...]
    ppermute x8 -> x6, waiting for transfers between devices: 6.4 us -> 0.02 us  [ring(): lax.ppermute(value, axis, [(i, (i + steps) % count) for i in range(count)])]
    pallas_call x2, Pallas kernels: 16.9 us -> 12 us  [the longest x1 6.83 us: per_device(): call(kern(forward_kernel), sd((F, 6 * CP, C), F32), [VM, VM, VM, VM], [pl...]
    ppermute x0 -> x2, waiting for transfers between devices: none -> 1.27 us  [swap(): lax.ppermute(value, 'tile', [(at, to % tiles) for at, to in enumerate(pla...]
    unnamed x12 -> x10, local copies, waits for them, and re-layouts: 1.6 us -> 0.64 us
  transfers between devices with their start and end apart: 8 -> 8, of which waited for: 2 -> 1; matrix products, arithmetic and copies ran while one was open for 1% -> 1% of each run, Pallas kernels for 43% -> 43%
where the time goes in v2:
time: 55.6 us; the launch traced here: 55.4 us
  Pallas kernels  26.7 us (48%)
  starting transfers between devices  22.6 us (41%)
  local copies, waits for them, and re-layouts  3.59 us (6%)
  waiting for transfers between devices  1.29 us (2%)
  between operations  0.8 us (1%)
    ppermute x6, starting transfers between devices, ring(): lax.ppermute(value, axis, [(i, (i + steps) % count) for i in range(count)])  14.7 us
    pallas_call x1, Pallas kernels, per_device(): call(back_kernel, (sd((F, 8 * BW, C), F32), sd((2, 8 * BW, C), BF)), [VM,...  8.59 us
    ppermute x2, starting transfers between devices, swap(): lax.ppermute(value, 'tile', [(at, to % tiles) for at, to in enumerate(pla...  7.84 us
    pallas_call x1, Pallas kernels, per_device(): call(kern(forward_kernel), sd((F, 6 * CP, C), F32), [VM, VM, VM, VM], [pl...  6.83 us
    pallas_call x1, Pallas kernels, per_device(): call(kern(decode_kernel), sd((F, 2 * BR, BW, C), BF), [SM, VM, VM, VM, VM...  5.19 us
    pallas_call x1, Pallas kernels, per_device(): call(kern(grad_hidden_kernel), (sd((F, 6, CP, C), BF), sd((2, 2 * C, 2 *...  2.63 us
    slice x2, local copies, waits for them, and re-layouts, strip(): return jnp.concatenate([lat[:, :, a:a + 2], pg[:, :, a:a + 2]], 1)  2.13 us
    pallas_call x1, Pallas kernels, per_device(): call(kern(latent_grad_kernel), sd((F, BR, BW, C), F32), [SM, VM, VM, VM,...  1.82 us
  transfers between devices with their start and end apart: 8, of which 1 were waited for; matrix products, arithmetic and copies ran while one was open for 1% of the time, Pallas kernels for 43%

profile of v2, /device:TPU:6, one launch (start us, length us, event | category | flops | bytes accessed | tf_op | source)
XLA Modules:
  0.0 55.4 jit_solution(13387290481132823462)
XLA Ops:
  0.6 0.0 copy-start
  0.6 1.0 %fusion.2 = (bf16[4,4,2,384]{3,2,1,0:T(2,128)(2,1)S(1)}, bf16[4,4,2,384]{3,2,1,0:T(2,128)(2,1)S(1)}) fusion(bf16[4,4,24,384]{3,2,1,0:T(8,128)(2,1)} %bitcast.14), kind=kLoop, calls=%fused_computation.9 | loop fusion | bytes 98304 | tf_op jit(solution)/shard_map/slice | solution.py:292
  1.7 1.1 %fusion = (bf16[4,8,2,384]{3,2,1,0:T(2,128)(2,1)S(1)}, bf16[4,8,2,384]{3,2,1,0:T(2,128)(2,1)S(1)}) fusion(bf16[4,8,24,384]{3,2,1,0:T(8,128)(2,1)} %bitcast.17), kind=kLoop, calls=%fused_computation.7 | loop fusion | bytes 196608 | tf_op jit(solution)/shard_map/slice | solution.py:292
  2.8 0.2 broadcast_select_fusion.3
  3.0 0.0 copy-start.1
  3.0 0.0 copy-start.2
  3.0 0.0 copy-start.4
  3.0 7.8 %collective-permute-start = (bf16[4,12,2,384]{3,2,1,0:T(2,128)(2,1)S(1)}, bf16[4,12,2,384]{3,2,1,0:T(2,128)(2,1)S(1)}, u32[]{:S(2)}, u32[]{:S(2)}) collective-permute-start(bf16[4,12,2,384]{3,2,1,0:T(2,128)(2,1)S(1)} %get-tuple-element.30), channel_id=1, source_target_pairs={{0,63},{1,2},{2,1},{3,4},{4,3},{5,6},{6,5},{7,8},{8,7},{9,10},{10,... | collective-permute-start | bytes 221192 | tf_op jit(solution)/shard_map/ppermute | solution.py:277
  10.9 0.0 collective-permute-start.1
  10.9 0.7 %reshape.10.gain = f32[1,384]{1,0:T(1,128)S(1)} reshape(f32[384]{0:T(512)} %param.8) | data formatting | bytes 3072 | tf_op jit(solution)/shard_map/reshape | solution.py:283
  11.6 0.1 pad.1.clone
  11.6 1.3 %collective-permute-done = bf16[4,12,2,384]{3,2,1,0:T(2,128)(2,1)S(1)} collective-permute-done((bf16[4,12,2,384]{3,2,1,0:T(2,128)(2,1)S(1)}, bf16[4,12,2,384]{3,2,1,0:T(2,128)(2,1)S(1)}, u32[]{:S(2)}, u32[]{:S(2)}) %collective-permute-start) | collective-permute-done | bytes 73760 | tf_op jit(solution)/shard_map/ppermute | solution.py:277
  12.9 0.0 collective-permute-done.1
  12.9 0.2 pad_maximum_fusion.halo
  13.1 0.0 copy-done
  13.2 0.3 shard_map.77.own
  13.5 0.1 collective-permute-start.2
  13.6 5.6 %collective-permute-start.3 = (bf16[4,2,32,384]{3,2,1,0:T(8,128)(2,1)S(1)}, bf16[4,2,32,384]{3,2,1,0:T(8,128)(2,1)S(1)}, u32[]{:S(2)}, u32[]{:S(2)}) collective-permute-start(bf16[4,2,32,384]{3,2,1,0:T(8,128)(2,1)S(1)} %get-tuple-element.24), channel_id=1, source_target_pairs={{0,60},{1,61},{2,62},{3,63},{4,0},{5,1},{6,2},{7,3},{8,4},{9,5},{1... | collective-permute-start | bytes 589832 | tf_op jit(solution)/shard_map/ppermute | solution.py:272
  19.2 0.0 copy-done.1
  19.2 0.0 copy-done.2
  19.2 0.0 copy-done.4
  19.2 0.0 copy-start.3
  19.2 2.6 %shard_map.79 = (bf16[4,6,32,384]{3,2,1,0:T(8,128)(2,1)S(1)}, bf16[2,768,768]{2,1,0:T(8,128)(2,1)S(1)}) custom-call(s32[4]{0:T(128)S(1)} %copy-done.2, bf16[4,8,24,384]{3,2,1,0:T(8,128)(2,1)S(1)} %bitcast.18, bf16[4,12,8,384]{3,2,1,0:T(8,128)(2,1)S(1)} %pad_maximum_fusion.halo, bf16[3,3,192,384]{3,2,1,0:T(8,128)(2,1)S(1)} %bitcast.21, ...), custom_call_target="tpu_custom_call" | custom-call | flops 3000000000 | bytes 1000000 | tf_op jit(solution)/shard_map/pallas_call | solution.py:302
  21.8 0.6 %copy-done.3 = bf16[3,3,3,384,384]{4,3,2,1,0:T(8,128)(2,1)S(1)} copy-done((bf16[3,3,3,384,384]{4,3,2,1,0:T(8,128)(2,1)S(1)}, bf16[3,3,3,384,384]{4,3,2,1,0:T(8,128)(2,1)}, u32[]{:S(2)}) %copy-start.3) | copy-done | bytes 7962648
  22.5 8.6 %shard_map.80 = (f32[4,192,384]{2,1,0:T(8,128)S(1)}, bf16[2,192,384]{2,1,0:T(8,128)(2,1)S(1)}) custom-call(bf16[4,6,32,384]{3,2,1,0:T(8,128)(2,1)S(1)} %get-tuple-element.11.gh, bf16[3,3,3,384,384]{4,3,2,1,0:T(8,128)(2,1)S(1)} %copy-done.3), custom_call_target="tpu_custom_call" | custom-call | flops 6000000000 | bytes 1000000 | tf_op jit(solution)/shard_map/pallas_call | solution.py:309
  31.1 0.0 collective-permute-done.2.above
  31.1 0.0 collective-permute-done.3.below
  31.1 0.6 %shard_map.81 = (bf16[2,8,32,384]{3,2,1,0:T(8,128)(2,1)S(1)}, bf16[2,192,384]{2,1,0:T(8,128)(2,1)S(1)}) custom-call(s32[4]{0:T(128)S(1)} %copy-done.2, bf16[4,4,32,384]{3,2,1,0:T(8,128)(2,1)S(1)} %shard_map.77.own, bf16[4,2,32,384]{3,2,1,0:T(8,128)(2,1)S(1)} %collective-permute-done.2.above, bf16[4,2,32,384]{3,2,1,0:T(8,128)(2,1)S(1)} %collective-permute-done.3.below, ...), custom_call_target="tpu_custom_call" | custom-call | bytes 1000000 | tf_op jit(solution)/shard_map/pallas_call | solution.py:321
  31.7 0.9 %collective-permute-start.5 = (bf16[2,192,384]{2,1,0:T(8,128)(2,1)S(1)}, bf16[2,192,384]{2,1,0:T(8,128)(2,1)S(1)}, u32[]{:S(2)}, u32[]{:S(2)}) collective-permute-start(bf16[2,192,384]{2,1,0:T(8,128)(2,1)S(1)} %get-tuple-element.16), channel_id=1, source_target_pairs={{0,192},{64,0},{128,64},{192,128},{1,193},{65,1},{129,65},{193,129... | collective-permute-start | bytes 884744 | tf_op jit(solution)/shard_map/ppermute | solution.py:272
  32.6 2.4 %collective-permute-start.4 = (bf16[2,8,32,384]{3,2,1,0:T(8,128)(2,1)S(1)}, bf16[2,8,32,384]{3,2,1,0:T(8,128)(2,1)S(1)}, u32[]{:S(2)}, u32[]{:S(2)}) collective-permute-start(bf16[2,8,32,384]{3,2,1,0:T(8,128)(2,1)S(1)} %get-tuple-element.13), channel_id=1, source_target_pairs={{0,64},{64,128},{128,192},{192,0},{1,65},{65,129},{129,193},{193,1... | collective-permute-start | bytes 1179656 | tf_op jit(solution)/shard_map/ppermute | solution.py:272
  35.0 6.8 %shard_map.78.part = f32[4,192,384]{2,1,0:T(8,128)S(1)} custom-call(bf16[4,4,32,384]{3,2,1,0:T(8,128)(2,1)S(1)} %shard_map.77.own, bf16[4,2,32,384]{3,2,1,0:T(8,128)(2,1)S(1)} %collective-permute-done.2.above, bf16[4,2,32,384]{3,2,1,0:T(8,128)(2,1)S(1)} %collective-permute-done.3.below, bf16[3,3,1152,384]{3,2,1,0:T(8,128)(2,1)S(1)} %bitcast.19), custom_call_target="tpu_custom_call" | custom-call | flops 6000000000 | bytes 1000000 | tf_op jit(solution)/shard_map/pallas_call | solution.py:328
  41.9 0.0 collective-permute-done.5.later
  41.9 0.8 %shard_map.83 = (bf16[4,48,384]{2,1,0:T(8,128)(2,1)S(1)}, bf16[4,48,384]{2,1,0:T(8,128)(2,1)S(1)}, f32[4,96,384]{2,1,0:T(8,128)S(1)}) custom-call(s32[4]{0:T(128)S(1)} %copy-done.2, f32[4,192,384]{2,1,0:T(8,128)S(1)} %get-tuple-element.15.acc, bf16[2,192,384]{2,1,0:T(8,128)(2,1)S(1)} %collective-permute-done.5.later), custom_call_target="tpu_custom_call" | custom-call | bytes 1000000 | tf_op jit(solution)/shard_map/pallas_call | solution.py:335
  42.6 0.1 collective-permute-start.6
  42.7 5.6 %collective-permute-start.7 = (bf16[4,48,384]{2,1,0:T(8,128)(2,1)S(1)}, bf16[4,48,384]{2,1,0:T(8,128)(2,1)S(1)}, u32[]{:S(2)}, u32[]{:S(2)}) collective-permute-start(bf16[4,48,384]{2,1,0:T(8,128)(2,1)S(1)} %get-tuple-element.19), channel_id=1, source_target_pairs={{0,60},{1,61},{2,62},{3,63},{4,0},{5,1},{6,2},{7,3},{8,4},{9,5},{1... | collective-permute-start | bytes 442376 | tf_op jit(solution)/shard_map/ppermute | solution.py:272
  48.4 0.0 collective-permute-done.4.prior
  48.4 5.2 %shard_map.82 = bf16[4,8,24,384]{3,2,1,0:T(8,128)(2,1)} custom-call(s32[4]{0:T(128)S(1)} %copy-done.2, f32[4,192,384]{2,1,0:T(8,128)S(1)} %shard_map.78.part, bf16[2,8,32,384]{3,2,1,0:T(8,128)(2,1)S(1)} %collective-permute-done.4.prior, bf16[3,3,1152,384]{3,2,1,0:T(8,128)(2,1)S(1)} %bitcast.20, bf16[2,768,768]{2,1,0:T(8,128)(2,1)S(1)} %get-tuple-element.14.upw), custom_call_target="tpu_custom_call" | custom-call | flops 4000000000 | bytes 1000000 | tf_op jit(solution)/shard_map/pallas_call | solution.py:343
  53.6 0.0 collective-permute-done.6.above
  53.6 0.0 collective-permute-done.7.below
  53.6 1.8 %shard_map.84 = f32[4,4,24,384]{3,2,1,0:T(8,128)} custom-call(s32[4]{0:T(128)S(1)} %copy-done.2, bf16[4,4,24,384]{3,2,1,0:T(8,128)(2,1)S(1)} %bitcast.16, f32[1,384]{1,0:T(1,128)S(1)} %reshape.10.gain, f32[4,96,384]{2,1,0:T(8,128)S(1)} %get-tuple-element.17.own, bf16[4,48,384]{2,1,0:T(8,128)(2,1)S(1)} %collective-permute-done.6.above, ...), custom_call_target="tpu_custom_call" | custom-call | bytes 1000000 | tf_op jit(solution)/shard_map/pallas_call | solution.py:353
  (3 shorter events, 0.1 us)
Async XLA Ops:
  0.6 12.5 %copy-start = (bf16[4,1,4,24,384]{4,3,2,1,0:T(8,128)(2,1)S(1)}, bf16[4,1,4,24,384]{4,3,2,1,0:T(8,128)(2,1)}, u32[]{:S(2)}) copy-start(bf16[4,1,4,24,384]{4,3,2,1,0:T(8,128)(2,1)} %param.6) | copy-start | bytes 884740
  3.0 16.2 %copy-start.1 = (bf16[4,1,8,24,384]{4,3,2,1,0:T(8,128)(2,1)S(1)}, bf16[4,1,8,24,384]{4,3,2,1,0:T(8,128)(2,1)}, u32[]{:S(2)}) copy-start(bf16[4,1,8,24,384]{4,3,2,1,0:T(8,128)(2,1)} %param.11) | copy-start | bytes 1769476
  3.0 16.2 %copy-start.2 = (s32[4]{0:T(128)S(1)}, s32[4]{0:T(128)}, u32[]{:S(2)}) copy-start(s32[4]{0:T(128)} %counts.9) | copy-start | bytes 52
  3.0 16.2 %copy-start.4 = (bf16[3,3,384,192]{2,3,1,0:T(8,128)(2,1)S(1)}, bf16[3,3,384,192]{2,3,1,0:T(8,128)(2,1)}, u32[]{:S(2)}) copy-start(bf16[3,3,384,192]{2,3,1,0:T(8,128)(2,1)} %param.10) | copy-start | bytes 3981316
  3.0 9.9 %collective-permute-start = (bf16[4,12,2,384]{3,2,1,0:T(2,128)(2,1)S(1)}, bf16[4,12,2,384]{3,2,1,0:T(2,128)(2,1)S(1)}, u32[]{:S(2)}, u32[]{:S(2)}) collective-permute-start(bf16[4,12,2,384]{3,2,1,0:T(2,128)(2,1)S(1)} %get-tuple-element.30), channel_id=1, source_target_pairs={{0,63},{1,2},{2,1},{3,4},{4,3},{5,6},{6,5},{7,8},{8,7},{9,10},{10,... | collective-permute-start | bytes 221192 | tf_op jit(solution)/shard_map/ppermute | solution.py:277
  10.9 2.0 %collective-permute-start.1 = (bf16[4,12,2,384]{3,2,1,0:T(2,128)(2,1)S(1)}, bf16[4,12,2,384]{3,2,1,0:T(2,128)(2,1)S(1)}, u32[]{:S(2)}, u32[]{:S(2)}) collective-permute-start(bf16[4,12,2,384]{3,2,1,0:T(2,128)(2,1)S(1)} %get-tuple-element.31), channel_id=1, source_target_pairs={{0,1},{1,0},{2,3},{3,2},{4,5},{5,4},{6,7},{7,6},{8,9},{9,8},{10,11... | collective-permute-start | bytes 221192 | tf_op jit(solution)/shard_map/ppermute | solution.py:277
  13.5 17.6 %collective-permute-start.2 = (bf16[4,2,32,384]{3,2,1,0:T(8,128)(2,1)S(1)}, bf16[4,2,32,384]{3,2,1,0:T(8,128)(2,1)S(1)}, u32[]{:S(2)}, u32[]{:S(2)}) collective-permute-start(bf16[4,2,32,384]{3,2,1,0:T(8,128)(2,1)S(1)} %get-tuple-element.25), channel_id=1, source_target_pairs={{0,4},{1,5},{2,6},{3,7},{4,8},{5,9},{6,10},{7,11},{8,12},{9,13},{1... | collective-permute-start | bytes 589832 | tf_op jit(solution)/shard_map/ppermute | solution.py:272
  13.6 17.5 %collective-permute-start.3 = (bf16[4,2,32,384]{3,2,1,0:T(8,128)(2,1)S(1)}, bf16[4,2,32,384]{3,2,1,0:T(8,128)(2,1)S(1)}, u32[]{:S(2)}, u32[]{:S(2)}) collective-permute-start(bf16[4,2,32,384]{3,2,1,0:T(8,128)(2,1)S(1)} %get-tuple-element.24), channel_id=1, source_target_pairs={{0,60},{1,61},{2,62},{3,63},{4,0},{5,1},{6,2},{7,3},{8,4},{9,5},{1... | collective-permute-start | bytes 589832 | tf_op jit(solution)/shard_map/ppermute | solution.py:272
  19.2 3.3 %copy-start.3 = (bf16[3,3,3,384,384]{4,3,2,1,0:T(8,128)(2,1)S(1)}, bf16[3,3,3,384,384]{4,3,2,1,0:T(8,128)(2,1)}, u32[]{:S(2)}) copy-start(bf16[3,3,3,384,384]{4,3,2,1,0:T(8,128)(2,1)} %weight.1) | copy-start | bytes 23887876
  31.7 10.2 %collective-permute-start.5 = (bf16[2,192,384]{2,1,0:T(8,128)(2,1)S(1)}, bf16[2,192,384]{2,1,0:T(8,128)(2,1)S(1)}, u32[]{:S(2)}, u32[]{:S(2)}) collective-permute-start(bf16[2,192,384]{2,1,0:T(8,128)(2,1)S(1)} %get-tuple-element.16), channel_id=1, source_target_pairs={{0,192},{64,0},{128,64},{192,128},{1,193},{65,1},{129,65},{193,129... | collective-permute-start | bytes 884744 | tf_op jit(solution)/shard_map/ppermute | solution.py:272
  32.6 15.7 %collective-permute-start.4 = (bf16[2,8,32,384]{3,2,1,0:T(8,128)(2,1)S(1)}, bf16[2,8,32,384]{3,2,1,0:T(8,128)(2,1)S(1)}, u32[]{:S(2)}, u32[]{:S(2)}) collective-permute-start(bf16[2,8,32,384]{3,2,1,0:T(8,128)(2,1)S(1)} %get-tuple-element.13), channel_id=1, source_target_pairs={{0,64},{64,128},{128,192},{192,0},{1,65},{65,129},{129,193},{193,1... | collective-permute-start | bytes 1179656 | tf_op jit(solution)/shard_map/ppermute | solution.py:272
  42.6 10.9 %collective-permute-start.6 = (bf16[4,48,384]{2,1,0:T(8,128)(2,1)S(1)}, bf16[4,48,384]{2,1,0:T(8,128)(2,1)S(1)}, u32[]{:S(2)}, u32[]{:S(2)}) collective-permute-start(bf16[4,48,384]{2,1,0:T(8,128)(2,1)S(1)} %get-tuple-element.18), channel_id=1, source_target_pairs={{0,4},{1,5},{2,6},{3,7},{4,8},{5,9},{6,10},{7,11},{8,12},{9,13},{1... | collective-permute-start | bytes 442376 | tf_op jit(solution)/shard_map/ppermute | solution.py:272
  42.7 10.8 %collective-permute-start.7 = (bf16[4,48,384]{2,1,0:T(8,128)(2,1)S(1)}, bf16[4,48,384]{2,1,0:T(8,128)(2,1)S(1)}, u32[]{:S(2)}, u32[]{:S(2)}) collective-permute-start(bf16[4,48,384]{2,1,0:T(8,128)(2,1)S(1)} %get-tuple-element.19), channel_id=1, source_target_pairs={{0,60},{1,61},{2,62},{3,63},{4,0},{5,1},{6,2},{7,3},{8,4},{9,5},{1... | collective-permute-start | bytes 442376 | tf_op jit(solution)/shard_map/ppermute | solution.py:272

commit v3 on v2

--- a/solution.py
+++ b/solution.py
@@ -26,6 +26,8 @@
         section=section,
         up=row > 0,
         down=row < tiles // GCOL - 1,
+        first_below=lax.rem(row, 2) == 0,
+        first_left=lax.rem(col, 2) == 0,
         left=col > 0,
         right=col < GCOL - 1,
         before=section > 0,
@@ -51,15 +53,49 @@
     return pltpu.roll(x, (-by) % CP, axis=x.ndim - 2)
 
 
-def acts_kernel(sizes, lat, halo, gain, out):
+def strips_kernel(sizes, lat, pg, one, two):
+    even = place_of(sizes)["first_left"]
+    for f in range(F):
+        for source, base in ((lat, 0), (pg, BR * F)):
+            rows = source.shape[1]
+            first = source[f, :, 0:8].astype(F32)
+            last = source[f, :, BW - 8 : BW].astype(F32)
+            for k in range(2):
+                a, b = first[:, k], last[:, 6 + k]
+                to = slice(base + f * rows, base + (f + 1) * rows)
+                one[k, to] = jnp.where(even, b, a).astype(BF)
+                two[k, to] = jnp.where(even, a, b).astype(BF)
+
+
+def side_columns(where, one, two, base, rows):
+    even = where["first_left"]
+    column = lax.broadcasted_iota(jnp.int32, (1, 8, C), 1)
+    whole = jnp.zeros((rows, 8, C), F32)
+    for k in range(2):
+        a = one[k, base : base + rows].astype(F32)[:, None]
+        b = two[k, base : base + rows].astype(F32)[:, None]
+        whole = jnp.where(column == k, jnp.where(even, a, b), whole)
+        whole = jnp.where(column == 6 + k, jnp.where(even, b, a), whole)
+    return whole
+
+
+def acts_kernel(sizes, lat, side_one, side_two, gain, out, one, two):
     where = place_of(sizes)
     mask = column_mask(where, C, 2)
     g = gain[...].reshape(1, 1, C)
     for f in range(F):
-        whole = jnp.concatenate(
-            [lat[f].astype(F32), halo[f, 0:BR].astype(F32)], axis=1
-        )
+        side = side_columns(where, side_one, side_two, f * BR, BR)
+        whole = jnp.concatenate([lat[f].astype(F32), side], axis=1)
         out[f] = jnp.where(mask, activate(whole, g), 0.0).astype(BF)
+    start = jnp.where(where["first_below"], 2, 0)
+    for f in range(F):
+        one[f] = out[f, pl.ds(start, 2)]
+        two[f] = out[f, pl.ds(2 - start, 2)]
+
+
+def from_rows(where, one, two):
+    below = where["first_below"]
+    return jnp.where(below, two, one), jnp.where(below, one, two)
 
 
 def up_taps(up, upw):
@@ -73,17 +109,16 @@
                 upw[k, b * (C // 2) : (b + 1) * (C // 2), a * C : (a + 1) * C] = total.astype(BF)
 
 
-def grad_hidden_kernel(sizes, counts, pg, halo, up, own, out, upw, parts, acc):
+def grad_hidden_kernel(sizes, counts, pg, rim_one, rim_two, up, own, out, upw, parts, acc):
     where = place_of(sizes)
     up_taps(up, upw)
     length = counts[where["section"]]
     mask = column_mask(where, C, 2)
     low = lax.broadcasted_iota(jnp.int32, (1, CP, C), 2) < C // 2
     for f in range(F):
+        side = side_columns(where, rim_one, rim_two, BR * F + f * 2 * BR, 2 * BR)
         for r in range(0, 2 * BR, 2):
-            whole = jnp.concatenate(
-                [pg[f, r : r + 2].astype(F32), halo[f, BR + r : BR + r + 2].astype(F32)], axis=1
-            )
+            whole = jnp.concatenate([pg[f, r : r + 2].astype(F32), side[r : r + 2]], axis=1)
             whole = jnp.where(mask & (f < length), whole, 0.0)
             mix = jnp.where(low, shifted(whole, 1), shifted(whole, -1))
             for k in range(2):
@@ -110,18 +145,7 @@
         out[f] = jnp.where(keep, value, 0.0).astype(BF)
 
 
-def back_kernel(gh, weight, acc_out, early_out, wt, cells, acc, sems):
-    copies = {}
-    for dt in (2, 1, 0):
-        for dr in range(3):
-            for dc in range(3):
-                copy = pltpu.make_async_copy(
-                    weight.at[dt, dr, dc],
-                    wt.at[dt, dr * C : (dr + 1) * C, dc * C : (dc + 1) * C],
-                    sems.at[dt * 9 + dr * 3 + dc],
-                )
-                copy.start()
-                copies[dt, dr, dc] = copy
+def back_kernel(gh, weight, acc_out, early_out, cells, acc):
     for f in range(F):
         value = gh[f].astype(F32)
         for dc in range(3):
@@ -130,12 +154,16 @@
     acc[...] = jnp.zeros(acc.shape, F32)
     left = cells[...].reshape(F * 6 * BW, 3 * C)
     for dt in (2, 1, 0):
+        taps = jnp.concatenate(
+            [
+                jnp.concatenate([weight[dt, dr, dc] for dc in range(3)], axis=1)
+                for dr in range(3)
+            ],
+            axis=0,
+        )
+        product = lax.dot_general(left, taps, NT, preferred_element_type=F32)
         for dr in range(3):
-            for dc in range(3):
-                copies[dt, dr, dc].wait()
-        product = lax.dot_general(left, wt[dt], NT, preferred_element_type=F32)
-        for f in range(F):
-            for dr in range(3):
+            for f in range(F):
                 acc[f + dt, dr * BW : (dr + 6) * BW] += product[
                     f * 6 * BW : (f + 1) * 6 * BW, dr * C : (dr + 1) * C
                 ]
@@ -143,15 +171,15 @@
     acc_out[...] = acc[2:6]
 
 
-def edge_frames_kernel(sizes, counts, own, above, below, early, out, early_out):
-    early_out[...] = early[...]
+def edge_frames_kernel(sizes, counts, own, one, two, early, out):
     where = place_of(sizes)
     length = counts[where["section"]]
     for k in range(2):
         f = length - 2 + k
-        out[k, 0:2] = jnp.where(where["up"], above[f], jnp.zeros((2, CP, C), BF))
+        above, below = from_rows(where, one[f], two[f])
+        out[k, 0:2] = jnp.where(where["up"], above, jnp.zeros((2, CP, C), BF))
         out[k, 2:6] = own[f]
-        out[k, 6:8] = jnp.where(where["down"], below[f], jnp.zeros((2, CP, C), BF))
+        out[k, 6:8] = jnp.where(where["down"], below, jnp.zeros((2, CP, C), BF))
 
 
 def side_by_side(x, rows, cells, f):
@@ -163,27 +191,43 @@
         ).astype(BF)
 
 
-def forward_kernel(sizes, own, above, below, weight, acc_out, cells):
-    where = place_of(sizes)
-    for f in range(F):
-        side_by_side(jnp.where(where["up"], above[f].astype(F32), 0.0), 0, cells, f)
-        side_by_side(own[f].astype(F32), 2, cells, f)
-        side_by_side(jnp.where(where["down"], below[f].astype(F32), 0.0), 6, cells, f)
+def forward_own_kernel(own, weight, edge, acc, cells):
+    for f in range(F):
+        side_by_side(own[f].astype(F32), 0, cells, f)
+    acc[...] = jnp.zeros(acc.shape, F32)
     for dt in (2, 1, 0):
         count = F - (2 - dt)
-        total = None
+        taps = jnp.concatenate([weight[dt, dr] for dr in range(3)], axis=1)
+        left = cells[0:count].reshape(count * BR * CP, 3 * C)
+        product = jnp.dot(left, taps, preferred_element_type=F32)
         for dr in range(3):
-            left = cells[0:count, dr * CP : (dr + 6) * CP].reshape(count * 6 * CP, 3 * C)
+            for f in range(count):
+                acc[f + 2 - dt, (2 - dr) * CP : (6 - dr) * CP] += product[
+                    f * BR * CP : (f + 1) * BR * CP, dr * C : (dr + 1) * C
+                ]
+
+
+def forward_rim_kernel(sizes, one, two, part, weight, mine, acc, cells):
+    where = place_of(sizes)
+    for f in range(F):
+        above, below = from_rows(where, one[f].astype(F32), two[f].astype(F32))
+        side_by_side(jnp.where(where["up"], above, 0.0), 0, cells, f)
+        side_by_side(jnp.where(where["down"], below, 0.0), 2, cells, f)
+    acc[...] = part[...]
+    for dt in (2, 1, 0):
+        count = F - (2 - dt)
+        terms = []
+        for dr in range(3):
+            left = cells[0:count, dr * CP : (dr + 2) * CP].reshape(count * 2 * CP, 3 * C)
             term = jnp.dot(left, weight[dt, dr], preferred_element_type=F32)
-            total = term if total is None else total + term
-        total = total.reshape(count, 6 * CP, C)
-        if dt == 2:
-            acc_out[...] = total
-        else:
-            acc_out[2 - dt : F] += total
-
-
-def decode_kernel(sizes, counts, part, prior, weight, upw, out, cells, pairs):
+            terms.append(term.reshape(count, 2 * CP, C))
+        acc[2 - dt : F, 0 : 2 * CP] += terms[0]
+        acc[2 - dt : F, 0:CP] += terms[1][:, 0:CP]
+        acc[2 - dt : F, 5 * CP : 6 * CP] += terms[1][:, CP : 2 * CP]
+        acc[2 - dt : F, 4 * CP : 6 * CP] += terms[2]
+
+
+def decode_kernel(sizes, counts, part, prior, weight, upw, out, mark, cells, pairs):
     where = place_of(sizes)
     length = counts[where["section"]]
     for k in range(2):
@@ -223,28 +267,32 @@
             value = jnp.where(f < length, whole[:, :, 0:C] + mix, 0.0)[:, 0:BW].astype(BF)
             for r in range(BR):
                 out[f, 2 * r + k] = value[r]
-
-
-def later_group_kernel(sizes, counts, acc, later, top, bottom, own, total):
+    mark[...] = jnp.zeros(mark.shape, F32)
+
+
+def later_group_kernel(sizes, counts, acc, later, one, two, own, total):
     where = place_of(sizes)
     length = counts[where["section"]]
     total[...] = acc[...]
     for k in range(2):
         f = length - 2 + k
         total[f] += jnp.where(where["after"], later[k].astype(F32), 0.0)
-    top[...] = total[:, 0 : 2 * BW].astype(BF)
-    bottom[...] = total[:, 6 * BW : 8 * BW].astype(BF)
+    top, bottom = total[:, 0 : 2 * BW], total[:, 6 * BW : 8 * BW]
+    below = where["first_below"]
+    one[...] = jnp.where(below, bottom, top).astype(BF)
+    two[...] = jnp.where(below, top, bottom).astype(BF)
     own[...] = total[:, 2 * BW : 6 * BW]
 
 
-def latent_grad_kernel(sizes, counts, lat, gain, own, above, below, out):
+def latent_grad_kernel(sizes, counts, lat, gain, own, one, two, mark, out):
     where = place_of(sizes)
     length = counts[where["section"]]
     g = gain[...].reshape(1, 1, C)
     for f in range(F):
         x = lat[f].astype(F32)
-        upper = own[f, 0 : 2 * BW] + jnp.where(where["up"], above[f].astype(F32), 0.0)
-        lower = own[f, 2 * BW : 4 * BW] + jnp.where(where["down"], below[f].astype(F32), 0.0)
+        above, below = from_rows(where, one[f].astype(F32), two[f].astype(F32))
+        upper = own[f, 0 : 2 * BW] + jnp.where(where["up"], above, 0.0)
+        lower = own[f, 2 * BW : 4 * BW] + jnp.where(where["down"], below, 0.0)
         grad = jnp.concatenate([upper, lower], 0).reshape(BR, BW, C)
         scale = lax.rsqrt(jnp.mean(x * x, axis=-1, keepdims=True) + EPS)
         unit = x * scale
@@ -255,13 +303,14 @@
         out[f] = jnp.where(f < length, scale * (t - unit * slope), 0.0)
 
 
-def call(kernel, outs, ins, scratch=(), flops=0, limit=40):
+def call(kernel, outs, ins, scratch=(), flops=0, limit=40, outs_at=None, aliases=None):
     return pl.pallas_call(
         kernel,
         out_shape=outs,
         in_specs=ins,
-        out_specs=jax.tree.map(lambda _: VM, outs),
+        out_specs=outs_at or jax.tree.map(lambda _: VM, outs),
         scratch_shapes=list(scratch),
+        input_output_aliases=aliases or {},
         compiler_params=pltpu.CompilerParams(vmem_limit_bytes=limit * 2**20),
         cost_estimate=pl.CostEstimate(flops=flops, bytes_accessed=1000000, transcendentals=0),
     )
@@ -272,9 +321,11 @@
     return lax.ppermute(value, axis, [(i, (i + steps) % count) for i in range(count)])
 
 
-def swap(value, tiles, shift):
-    places = [((at + GCOL + 1 + shift) ^ 1) - GCOL - 1 - shift for at in range(tiles)]
-    return lax.ppermute(value, "tile", [(at, to % tiles) for at, to in enumerate(places)])
+def swap(value, tiles, unit, second):
+    shift = GCOL + 1 + second * unit
+    return lax.ppermute(
+        value, "tile", [(at, (((at + shift) ^ unit) - shift) % tiles) for at in range(tiles)]
+    )
 
 
 def per_device(latents, counts, norm_gain, conv_weight, up_weight, pixel_grad):
@@ -286,63 +337,62 @@
     wide = conv_weight.reshape(3, 3, 3 * C, C)
 
     tiles = sizes[1]
-    even = lax.rem(lax.axis_index("tile") + GCOL + 1, 2) == 0
-
-    def strip(a):
-        return jnp.concatenate([lat[:, :, a : a + 2], pg[:, :, a : a + 2]], 1)
-
-    first, last = strip(0), strip(BW - 2)
-    one = swap(jnp.where(even, last, first), tiles, 0)
-    two = swap(jnp.where(even, first, last), tiles, 1)
-    from_left, from_right = jnp.where(even, two, one), jnp.where(even, one, two)
-    halo = jnp.concatenate([from_right, jnp.zeros((F, 3 * BR, 4, C), BF), from_left], 2)
-    own = call(kern(acts_kernel), sd((F, BR, CP, C), BF), [VM, VM, VM])(lat, halo, gain)
-    above = ring(own[:, 2:4], "tile", GCOL)
-    below = ring(own[:, 0:2], "tile", -GCOL)
+    side = sd((2, 3 * BR * F, C), BF)
+    side_one, side_two = call(kern(strips_kernel), (side, side), [VM, VM], flops=4 * 10**9)(lat, pg)
+    side_one, side_two = swap(side_one, tiles, 1, 0), swap(side_two, tiles, 1, 1)
+    rim = sd((F, 2, CP, C), BF)
+    own, one, two = call(
+        kern(acts_kernel), (sd((F, BR, CP, C), BF), rim, rim), [VM, VM, VM, VM], flops=4 * 10**9
+    )(lat, side_one, side_two, gain)
+    one, two = swap(one, tiles, GCOL, 0), swap(two, tiles, GCOL, 1)
     gh, upw = call(
         kern(grad_hidden_kernel),
         (sd((F, 6, CP, C), BF), sd((2, 2 * C, 2 * C), BF)),
-        [SM, VM, VM, VM, ANY],
+        [SM, VM, VM, VM, VM, ANY],
         [pltpu.VMEM((2, F, BR * CP, 2 * C), BF), pltpu.VMEM((F, 6 * CP, C), F32)],
         flops=3 * 10**9,
-    )(counts, pg, halo, jnp.transpose(up_weight, (0, 1, 3, 2)), own)
+    )(counts, pg, side_one, side_two, jnp.transpose(up_weight, (0, 1, 3, 2)), own)
     acc, early = call(
         back_kernel,
         (sd((F, 8 * BW, C), F32), sd((2, 8 * BW, C), BF)),
-        [VM, ANY],
+        [VM, VM],
         [
-            pltpu.VMEM((3, 3 * C, 3 * C), BF),
             pltpu.VMEM((F, 6 * BW, 3 * C), BF),
             pltpu.VMEM((F + 2, 8 * BW, C), F32),
-            pltpu.SemaphoreType.DMA((27,)),
         ],
         flops=6 * 10**9,
     )(gh, conv_weight)
-    edge, early = call(
-        kern(edge_frames_kernel),
-        (sd((2, 8, CP, C), BF), sd((2, 8 * BW, C), BF)),
-        [SM, VM, VM, VM, VM],
-    )(counts, own, above, below, early)
+    edge = call(
+        kern(edge_frames_kernel), sd((2, 8, CP, C), BF), [SM, VM, VM, VM, ANY]
+    )(counts, own, one, two, early)
     prior = ring(edge, "section", 1)
     later = ring(early, "section", -1)
+    partial = sd((F, 6 * CP, C), F32)
     part = call(
-        kern(forward_kernel),
-        sd((F, 6 * CP, C), F32),
-        [VM, VM, VM, VM],
-        [pltpu.VMEM((F, 8 * CP, 3 * C), BF)],
-        flops=6 * 10**9,
-    )(own, above, below, wide)
-    top, bottom, mine = call(
+        forward_own_kernel,
+        partial,
+        [VM, VM, ANY],
+        [pltpu.VMEM((F, BR * CP, 3 * C), BF)],
+        flops=4 * 10**9,
+    )(own, wide, edge)
+    rims = one, two
+    one, two, mine = call(
         kern(later_group_kernel),
         (sd((F, 2 * BW, C), BF), sd((F, 2 * BW, C), BF), sd((F, 4 * BW, C), F32)),
         [SM, VM, VM],
         [pltpu.VMEM((F, 8 * BW, C), F32)],
     )(counts, acc, later)
-    from_above = ring(bottom, "tile", GCOL)
-    from_below = ring(top, "tile", -GCOL)
-    decoded = call(
+    one, two = swap(one, tiles, GCOL, 0), swap(two, tiles, GCOL, 1)
+    part = call(
+        kern(forward_rim_kernel),
+        partial,
+        [VM, VM, VM, VM, ANY],
+        [pltpu.VMEM((F, BR * CP, 3 * C), BF)],
+        flops=3 * 10**9,
+    )(*rims, part, wide, mine)
+    decoded, mark = call(
         kern(decode_kernel),
-        sd((F, 2 * BR, BW, C), BF),
+        (sd((F, 2 * BR, BW, C), BF), sd((8, 128), F32)),
         [SM, VM, VM, VM, VM],
         [
             pltpu.VMEM((2, 8 * CP, 3 * C), BF),
@@ -351,8 +401,8 @@
         flops=4 * 10**9,
     )(counts, part, prior, wide, upw)
     grad = call(
-        kern(latent_grad_kernel), sd((F, BR, BW, C), F32), [SM, VM, VM, VM, VM, VM]
-    )(counts, lat, gain, mine, from_above, from_below)
+        kern(latent_grad_kernel), sd((F, BR, BW, C), F32), [SM, VM, VM, VM, VM, VM, ANY]
+    )(counts, lat, gain, mine, one, two, mark)
     return (decoded[:, None], grad[:, None])
 
 

time: 55.6 us -> 50 us (0.90)
  the two profiles are of different devices: /device:TPU:6 before, /device:TPU:1 now
where the time goes in v3:
time: 50 us; the launch traced here: 49.8 us
  Pallas kernels  24.6 us (49%)
  starting transfers between devices  19.4 us (39%)
  waiting for transfers between devices  3.02 us (6%)
  local copies, waits for them, and re-layouts  2.06 us (4%)
  between operations  0.78 us (2%)
    ppermute x6, starting transfers between devices, swap(): lax.ppermute(value, 'tile', [(at, ((at + shift ^ unit) - shift) % tiles)...  15.4 us
    pallas_call x1, Pallas kernels, per_device(): call(back_kernel, (sd((F, 8 * BW, C), F32), sd((2, 8 * BW, C), BF)), [VM,...  5.91 us
    pallas_call x1, Pallas kernels, per_device(): call(kern(decode_kernel), (sd((F, 2 * BR, BW, C), BF), sd((8, 128), F32))...  5.18 us
    pallas_call x1, Pallas kernels, per_device(): call(forward_own_kernel, partial, [VM, VM, ANY], [pltpu.VMEM((F, BR * CP,...  4.04 us
    ppermute x2, starting transfers between devices, ring(): lax.ppermute(value, axis, [(i, (i + steps) % count) for i in range(count)])  4.02 us
    ppermute x6, waiting for transfers between devices, swap(): lax.ppermute(value, 'tile', [(at, ((at + shift ^ unit) - shift) % tiles)...  3.01 us
    pallas_call x1, Pallas kernels, per_device(): call(kern(grad_hidden_kernel), (sd((F, 6, CP, C), BF), sd((2, 2 * C, 2 *...  2.84 us
    pallas_call x1, Pallas kernels, per_device(): call(kern(forward_rim_kernel), partial, [VM, VM, VM, VM, ANY], [pltpu.VME...  2.57 us
  transfers between devices with their start and end apart: 8, of which 3 were waited for; matrix products, arithmetic and copies ran while one was open for 0% of the time, Pallas kernels for 44%

profile of v3, /device:TPU:1, one launch (start us, length us, event | category | flops | bytes accessed | tf_op | source)
XLA Modules:
  0.0 49.8 jit_solution(9980690942446082260)
XLA Ops:
  0.6 0.0 copy-start
  0.6 1.0 %copy-done = bf16[4,1,4,24,384]{4,3,2,1,0:T(8,128)(2,1)S(1)} copy-done((bf16[4,1,4,24,384]{4,3,2,1,0:T(8,128)(2,1)S(1)}, bf16[4,1,4,24,384]{4,3,2,1,0:T(8,128)(2,1)}, u32[]{:S(2)}) %copy-start) | copy-done | bytes 294936
  1.6 0.0 copy-start.4
  1.6 1.1 %copy-done.4 = bf16[4,1,8,24,384]{4,3,2,1,0:T(8,128)(2,1)S(1)} copy-done((bf16[4,1,8,24,384]{4,3,2,1,0:T(8,128)(2,1)S(1)}, bf16[4,1,8,24,384]{4,3,2,1,0:T(8,128)(2,1)}, u32[]{:S(2)}) %copy-start.4) | copy-done | bytes 589848
  2.7 0.0 copy-start.6
  2.7 0.0 slice-start
  2.7 0.4 shard_map.77
  3.0 2.8 %collective-permute-start = (bf16[2,48,384]{2,1,0:T(8,128)(2,1)S(1)}, bf16[2,48,384]{2,1,0:T(8,128)(2,1)S(1)}, u32[]{:S(2)}, u32[]{:S(2)}) collective-permute-start(bf16[2,48,384]{2,1,0:T(8,128)(2,1)S(1)} %get-tuple-element.16), channel_id=1, source_target_pairs={{0,63},{1,2},{2,1},{3,4},{4,3},{5,6},{6,5},{7,8},{8,7},{9,10},{10,... | collective-permute-start | bytes 221192 | tf_op jit(solution)/shard_map/ppermute | solution.py:326
  5.8 6.6 %collective-permute-start.1 = (bf16[2,48,384]{2,1,0:T(8,128)(2,1)S(1)}, bf16[2,48,384]{2,1,0:T(8,128)(2,1)S(1)}, u32[]{:S(2)}, u32[]{:S(2)}) collective-permute-start(bf16[2,48,384]{2,1,0:T(8,128)(2,1)S(1)} %get-tuple-element.17), channel_id=1, source_target_pairs={{0,1},{1,0},{2,3},{3,2},{4,5},{5,4},{6,7},{7,6},{8,9},{9,8},{10,11... | collective-permute-start | bytes 221192 | tf_op jit(solution)/shard_map/ppermute | solution.py:326
  12.4 0.0 copy-done.6
  12.4 0.0 copy-start.2
  12.4 0.0 copy-start.3
  12.4 0.0 copy-start.5
  12.4 0.0 slice-start.1
  12.4 0.0 collective-permute-done.side_one.rim_one
  12.4 0.9 %collective-permute-done.1.side_two.rim_two = bf16[2,48,384]{2,1,0:T(8,128)(2,1)S(1)} collective-permute-done((bf16[2,48,384]{2,1,0:T(8,128)(2,1)S(1)}, bf16[2,48,384]{2,1,0:T(8,128)(2,1)S(1)}, u32[]{:S(2)}, u32[]{:S(2)}) %collective-permute-start.1) | collective-permute-done | bytes 73760 | tf_op jit(solution)/shard_map/ppermute | solution.py:326
  13.3 0.4 shard_map.78
  13.7 3.0 %collective-permute-start.2 = (bf16[4,2,32,384]{3,2,1,0:T(8,128)(2,1)S(1)}, bf16[4,2,32,384]{3,2,1,0:T(8,128)(2,1)S(1)}, u32[]{:S(2)}, u32[]{:S(2)}) collective-permute-start(bf16[4,2,32,384]{3,2,1,0:T(8,128)(2,1)S(1)} %get-tuple-element.18), channel_id=1, source_target_pairs={{0,60},{1,61},{2,62},{3,7},{4,8},{5,9},{6,10},{7,3},{8,4},{9,5},{1... | collective-permute-start | bytes 589832 | tf_op jit(solution)/shard_map/ppermute | solution.py:326
  16.7 0.0 collective-permute-start.3
  16.7 0.0 copy-done.2
  16.7 0.0 copy-done.3
  16.7 0.0 copy-done.5
  16.7 2.8 %shard_map.79 = (bf16[4,6,32,384]{3,2,1,0:T(8,128)(2,1)S(1)}, bf16[2,768,768]{2,1,0:T(8,128)(2,1)S(1)}) custom-call(s32[4]{0:T(128)S(1)} %copy-done.2, bf16[4,8,24,384]{3,2,1,0:T(8,128)(2,1)S(1)} %bitcast.20, bf16[2,48,384]{2,1,0:T(8,128)(2,1)S(1)} %collective-permute-done.side_one.rim_one, bf16[2,48,384]{2,1,0:T(8,128)(2,1)S(1)} %collective-permute-done.1.side_two.rim_two, ...), custom_call_target="tpu_custom_call" | custom-call | flops 3000000000 | bytes 1000000 | tf_op jit(solution)/shard_map/pallas_call | solution.py:348
  19.6 0.0 slice-done
  19.6 0.0 slice-done.1
  19.6 5.9 %shard_map.80 = (f32[4,192,384]{2,1,0:T(8,128)S(1)}, bf16[2,192,384]{2,1,0:T(8,128)(2,1)S(1)}) custom-call(bf16[4,6,32,384]{3,2,1,0:T(8,128)(2,1)S(1)} %get-tuple-element.21.gh, bf16[3,3,3,384,384]{4,3,2,1,0:T(8,128)(2,1)S(1)} %bitcast.11), custom_call_target="tpu_custom_call" | custom-call | flops 6000000000 | bytes 1000000 | tf_op jit(solution)/shard_map/pallas_call | solution.py:355
  25.5 2.6 %collective-permute-start.4 = (bf16[2,192,384]{2,1,0:T(8,128)(2,1)S(1)}, bf16[2,192,384]{2,1,0:T(8,128)(2,1)S(1)}, u32[]{:S(2)}, u32[]{:S(2)}) collective-permute-start(bf16[2,192,384]{2,1,0:T(8,128)(2,1)S(1)} %get-tuple-element.22.early), channel_id=1, source_target_pairs={{0,192},{64,0},{128,64},{192,128},{1,193},{65,1},{129,65},{193,129... | collective-permute-start | bytes 884744 | tf_op jit(solution)/shard_map/ppermute | solution.py:321
  28.1 0.0 collective-permute-done.2.one
  28.1 0.3 collective-permute-done.3.two
  28.4 0.6 %shard_map.81.edge = bf16[2,8,32,384]{3,2,1,0:T(8,128)(2,1)S(1)} custom-call(s32[4]{0:T(128)S(1)} %copy-done.2, bf16[4,4,32,384]{3,2,1,0:T(8,128)(2,1)S(1)} %get-tuple-element.20.own, bf16[4,2,32,384]{3,2,1,0:T(8,128)(2,1)S(1)} %collective-permute-done.2.one, bf16[4,2,32,384]{3,2,1,0:T(8,128)(2,1)S(1)} %collective-permute-done.3.two, ...), custom_call_target="tpu_custom_call" | custom-call | bytes 1000000 | tf_op jit(solution)/shard_map/pallas_call | solution.py:365
  29.0 1.5 %collective-permute-start.5 = (bf16[2,8,32,384]{3,2,1,0:T(8,128)(2,1)S(1)}, bf16[2,8,32,384]{3,2,1,0:T(8,128)(2,1)S(1)}, u32[]{:S(2)}, u32[]{:S(2)}) collective-permute-start(bf16[2,8,32,384]{3,2,1,0:T(8,128)(2,1)S(1)} %shard_map.81.edge), channel_id=1, source_target_pairs={{0,64},{64,128},{128,192},{192,0},{1,65},{65,129},{129,193},{193,1... | collective-permute-start | bytes 1179656 | tf_op jit(solution)/shard_map/ppermute | solution.py:321
  30.5 4.0 %shard_map.82.part = f32[4,192,384]{2,1,0:T(8,128)S(1)} custom-call(bf16[4,4,32,384]{3,2,1,0:T(8,128)(2,1)S(1)} %get-tuple-element.20.own, bf16[3,3,1152,384]{3,2,1,0:T(8,128)(2,1)S(1)} %bitcast.12, bf16[2,8,32,384]{3,2,1,0:T(8,128)(2,1)S(1)} %shard_map.81.edge), custom_call_target="tpu_custom_call" | custom-call | flops 4000000000 | bytes 1000000 | tf_op jit(solution)/shard_map/pallas_call | solution.py:371
  34.5 0.0 collective-permute-done.4.later
  34.6 0.8 %shard_map.83 = (bf16[4,48,384]{2,1,0:T(8,128)(2,1)S(1)}, bf16[4,48,384]{2,1,0:T(8,128)(2,1)S(1)}, f32[4,96,384]{2,1,0:T(8,128)S(1)}) custom-call(s32[4]{0:T(128)S(1)} %copy-done.2, f32[4,192,384]{2,1,0:T(8,128)S(1)} %get-tuple-element.23.acc, bf16[2,192,384]{2,1,0:T(8,128)(2,1)S(1)} %collective-permute-done.4.later), custom_call_target="tpu_custom_call" | custom-call | bytes 1000000 | tf_op jit(solution)/shard_map/pallas_call | solution.py:379
  35.4 3.0 %collective-permute-start.6 = (bf16[4,48,384]{2,1,0:T(8,128)(2,1)S(1)}, bf16[4,48,384]{2,1,0:T(8,128)(2,1)S(1)}, u32[]{:S(2)}, u32[]{:S(2)}) collective-permute-start(bf16[4,48,384]{2,1,0:T(8,128)(2,1)S(1)} %get-tuple-element.27), channel_id=1, source_target_pairs={{0,60},{1,61},{2,62},{3,7},{4,8},{5,9},{6,10},{7,3},{8,4},{9,5},{1... | collective-permute-start | bytes 442376 | tf_op jit(solution)/shard_map/ppermute | solution.py:326
  38.4 0.0 collective-permute-start.7
  38.4 2.6 %shard_map.84.part = f32[4,192,384]{2,1,0:T(8,128)S(1)} custom-call(bf16[4,2,32,384]{3,2,1,0:T(8,128)(2,1)S(1)} %collective-permute-done.2.one, bf16[4,2,32,384]{3,2,1,0:T(8,128)(2,1)S(1)} %collective-permute-done.3.two, f32[4,192,384]{2,1,0:T(8,128)S(1)} %shard_map.82.part, bf16[3,3,1152,384]{3,2,1,0:T(8,128)(2,1)S(1)} %bitcast.13, ...), custom_call_target="tpu_custom_call" | custom-call | flops 3000000000 | bytes 1000000 | tf_op jit(solution)/shard_map/pallas_call | solution.py:386
  41.0 0.0 collective-permute-done.5.prior
  41.0 0.0 copy-start.1
  41.0 5.2 %shard_map.85 = (bf16[4,8,24,384]{3,2,1,0:T(8,128)(2,1)}, f32[8,128]{1,0:T(8,128)S(1)}) custom-call(s32[4]{0:T(128)S(1)} %copy-done.2, f32[4,192,384]{2,1,0:T(8,128)S(1)} %shard_map.84.part, bf16[2,8,32,384]{3,2,1,0:T(8,128)(2,1)S(1)} %collective-permute-done.5.prior, bf16[3,3,1152,384]{3,2,1,0:T(8,128)(2,1)S(1)} %bitcast.14, ...), custom_call_target="tpu_custom_call" | custom-call | flops 4000000000 | bytes 1000000 | tf_op jit(solution)/shard_map/pallas_call | solution.py:393
  46.2 0.0 collective-permute-done.6.one
  46.2 1.8 %collective-permute-done.7.two = bf16[4,48,384]{2,1,0:T(8,128)(2,1)S(1)} collective-permute-done((bf16[4,48,384]{2,1,0:T(8,128)(2,1)S(1)}, bf16[4,48,384]{2,1,0:T(8,128)(2,1)S(1)}, u32[]{:S(2)}, u32[]{:S(2)}) %collective-permute-start.7) | collective-permute-done | bytes 147488 | tf_op jit(solution)/shard_map/ppermute | solution.py:326
  48.0 0.0 copy-done.1
  48.0 1.8 %shard_map.86 = f32[4,4,24,384]{3,2,1,0:T(8,128)} custom-call(s32[4]{0:T(128)S(1)} %copy-done.2, bf16[4,4,24,384]{3,2,1,0:T(8,128)(2,1)S(1)} %bitcast.17, f32[1,384]{1,0:T(1,128)S(1)} %reshape.10.gain, f32[4,96,384]{2,1,0:T(8,128)S(1)} %get-tuple-element.24.mine.own, bf16[4,48,384]{2,1,0:T(8,128)(2,1)S(1)} %collective-permute-done.6.one, ...), custom_call_target="tpu_custom_call" | custom-call | bytes 1000000 | tf_op jit(solution)/shard_map/pallas_call | solution.py:403
  (2 shorter events, 0.0 us)
Async XLA Ops:
  0.6 1.0 %copy-start = (bf16[4,1,4,24,384]{4,3,2,1,0:T(8,128)(2,1)S(1)}, bf16[4,1,4,24,384]{4,3,2,1,0:T(8,128)(2,1)}, u32[]{:S(2)}) copy-start(bf16[4,1,4,24,384]{4,3,2,1,0:T(8,128)(2,1)} %param.6) | copy-start | bytes 884740
  1.6 1.1 %copy-start.4 = (bf16[4,1,8,24,384]{4,3,2,1,0:T(8,128)(2,1)S(1)}, bf16[4,1,8,24,384]{4,3,2,1,0:T(8,128)(2,1)}, u32[]{:S(2)}) copy-start(bf16[4,1,8,24,384]{4,3,2,1,0:T(8,128)(2,1)} %param.11) | copy-start | bytes 1769476
  2.7 9.7 %copy-start.6 = (f32[384]{0:T(512)S(1)}, f32[384]{0:T(512)}, u32[]{:S(2)}) copy-start(f32[384]{0:T(512)} %param.8) | copy-start | bytes 4612
  2.7 16.9 %slice-start = ((s8[7962624]{0:T(1024)(128)(4,1)}), s8[4194304]{0:T(1024)(128)(4,1)S(1)}, s32[]{:S(2)}) async-start(s8[7962624]{0:T(1024)(128)(4,1)} %bitcast.10), calls=%async_computation | async-start | bytes 8388608
  3.0 9.4 %collective-permute-start = (bf16[2,48,384]{2,1,0:T(8,128)(2,1)S(1)}, bf16[2,48,384]{2,1,0:T(8,128)(2,1)S(1)}, u32[]{:S(2)}, u32[]{:S(2)}) collective-permute-start(bf16[2,48,384]{2,1,0:T(8,128)(2,1)S(1)} %get-tuple-element.16), channel_id=1, source_target_pairs={{0,63},{1,2},{2,1},{3,4},{4,3},{5,6},{6,5},{7,8},{8,7},{9,10},{10,... | collective-permute-start | bytes 221192 | tf_op jit(solution)/shard_map/ppermute | solution.py:326
  5.8 7.5 %collective-permute-start.1 = (bf16[2,48,384]{2,1,0:T(8,128)(2,1)S(1)}, bf16[2,48,384]{2,1,0:T(8,128)(2,1)S(1)}, u32[]{:S(2)}, u32[]{:S(2)}) collective-permute-start(bf16[2,48,384]{2,1,0:T(8,128)(2,1)S(1)} %get-tuple-element.17), channel_id=1, source_target_pairs={{0,1},{1,0},{2,3},{3,2},{4,5},{5,4},{6,7},{7,6},{8,9},{9,8},{10,11... | collective-permute-start | bytes 221192 | tf_op jit(solution)/shard_map/ppermute | solution.py:326
  12.4 4.3 %copy-start.2 = (s32[4]{0:T(128)S(1)}, s32[4]{0:T(128)}, u32[]{:S(2)}) copy-start(s32[4]{0:T(128)} %counts.9) | copy-start | bytes 52
  12.4 4.3 %copy-start.3 = (bf16[3,3,384,192]{2,3,1,0:T(8,128)(2,1)S(1)}, bf16[3,3,384,192]{2,3,1,0:T(8,128)(2,1)}, u32[]{:S(2)}) copy-start(bf16[3,3,384,192]{2,3,1,0:T(8,128)(2,1)} %param.10) | copy-start | bytes 3981316
  12.4 4.3 %copy-start.5 = (bf16[4,1,8,24,384]{4,3,2,1,0:T(8,128)(2,1)S(1)}, bf16[4,1,8,24,384]{4,3,2,1,0:T(8,128)(2,1)}, u32[]{:S(2)}) copy-start(bf16[4,1,8,24,384]{4,3,2,1,0:T(8,128)(2,1)} %param.11) | copy-start | bytes 1769476
  12.4 7.2 %slice-start.1 = ((s8[7962624]{0:T(1024)(128)(4,1)}), s8[3768320]{0:T(1024)(128)(4,1)S(1)}, s32[]{:S(2)}) async-start(s8[7962624]{0:T(1024)(128)(4,1)} %bitcast.10), calls=%async_computation.1 | async-start | bytes 7536640
  13.7 14.4 %collective-permute-start.2 = (bf16[4,2,32,384]{3,2,1,0:T(8,128)(2,1)S(1)}, bf16[4,2,32,384]{3,2,1,0:T(8,128)(2,1)S(1)}, u32[]{:S(2)}, u32[]{:S(2)}) collective-permute-start(bf16[4,2,32,384]{3,2,1,0:T(8,128)(2,1)S(1)} %get-tuple-element.18), channel_id=1, source_target_pairs={{0,60},{1,61},{2,62},{3,7},{4,8},{5,9},{6,10},{7,3},{8,4},{9,5},{1... | collective-permute-start | bytes 589832 | tf_op jit(solution)/shard_map/ppermute | solution.py:326
  16.7 11.7 %collective-permute-start.3 = (bf16[4,2,32,384]{3,2,1,0:T(8,128)(2,1)S(1)}, bf16[4,2,32,384]{3,2,1,0:T(8,128)(2,1)S(1)}, u32[]{:S(2)}, u32[]{:S(2)}) collective-permute-start(bf16[4,2,32,384]{3,2,1,0:T(8,128)(2,1)S(1)} %get-tuple-element.19), channel_id=1, source_target_pairs={{0,4},{1,5},{2,6},{3,63},{4,0},{5,1},{6,2},{7,11},{8,12},{9,13},{1... | collective-permute-start | bytes 589832 | tf_op jit(solution)/shard_map/ppermute | solution.py:326
  25.5 9.0 %collective-permute-start.4 = (bf16[2,192,384]{2,1,0:T(8,128)(2,1)S(1)}, bf16[2,192,384]{2,1,0:T(8,128)(2,1)S(1)}, u32[]{:S(2)}, u32[]{:S(2)}) collective-permute-start(bf16[2,192,384]{2,1,0:T(8,128)(2,1)S(1)} %get-tuple-element.22.early), channel_id=1, source_target_pairs={{0,192},{64,0},{128,64},{192,128},{1,193},{65,1},{129,65},{193,129... | collective-permute-start | bytes 884744 | tf_op jit(solution)/shard_map/ppermute | solution.py:321
  29.0 12.0 %collective-permute-start.5 = (bf16[2,8,32,384]{3,2,1,0:T(8,128)(2,1)S(1)}, bf16[2,8,32,384]{3,2,1,0:T(8,128)(2,1)S(1)}, u32[]{:S(2)}, u32[]{:S(2)}) collective-permute-start(bf16[2,8,32,384]{3,2,1,0:T(8,128)(2,1)S(1)} %shard_map.81.edge), channel_id=1, source_target_pairs={{0,64},{64,128},{128,192},{192,0},{1,65},{65,129},{129,193},{193,1... | collective-permute-start | bytes 1179656 | tf_op jit(solution)/shard_map/ppermute | solution.py:321
  35.4 10.8 %collective-permute-start.6 = (bf16[4,48,384]{2,1,0:T(8,128)(2,1)S(1)}, bf16[4,48,384]{2,1,0:T(8,128)(2,1)S(1)}, u32[]{:S(2)}, u32[]{:S(2)}) collective-permute-start(bf16[4,48,384]{2,1,0:T(8,128)(2,1)S(1)} %get-tuple-element.27), channel_id=1, source_target_pairs={{0,60},{1,61},{2,62},{3,7},{4,8},{5,9},{6,10},{7,3},{8,4},{9,5},{1... | collective-permute-start | bytes 442376 | tf_op jit(solution)/shard_map/ppermute | solution.py:326
  38.4 9.6 %collective-permute-start.7 = (bf16[4,48,384]{2,1,0:T(8,128)(2,1)S(1)}, bf16[4,48,384]{2,1,0:T(8,128)(2,1)S(1)}, u32[]{:S(2)}, u32[]{:S(2)}) collective-permute-start(bf16[4,48,384]{2,1,0:T(8,128)(2,1)S(1)} %get-tuple-element.28), channel_id=1, source_target_pairs={{0,4},{1,5},{2,6},{3,63},{4,0},{5,1},{6,2},{7,11},{8,12},{9,13},{1... | collective-permute-start | bytes 442376 | tf_op jit(solution)/shard_map/ppermute | solution.py:326
  41.0 7.0 %copy-start.1 = (bf16[4,1,4,24,384]{4,3,2,1,0:T(8,128)(2,1)S(1)}, bf16[4,1,4,24,384]{4,3,2,1,0:T(8,128)(2,1)}, u32[]{:S(2)}) copy-start(bf16[4,1,4,24,384]{4,3,2,1,0:T(8,128)(2,1)} %param.6) | copy-start | bytes 884740

commit v4 on v3

--- a/solution.py
+++ b/solution.py
@@ -89,8 +89,25 @@
         out[f] = jnp.where(mask, activate(whole, g), 0.0).astype(BF)
     start = jnp.where(where["first_below"], 2, 0)
     for f in range(F):
-        one[f] = out[f, pl.ds(start, 2)]
-        two[f] = out[f, pl.ds(2 - start, 2)]
+        one[f] = packed(out[f, pl.ds(start, 2)].astype(F32)).astype(BF)
+        two[f] = packed(out[f, pl.ds(2 - start, 2)].astype(F32)).astype(BF)
+
+
+def side_places():
+    place = lax.broadcasted_iota(jnp.int32, (8, C), 0)
+    return (place < 2) | (place >= 6)
+
+
+def packed(rows):
+    own = rows[:, 0:BW].reshape(2 * BW, C)
+    side = jnp.where(side_places(), rows[0, BW:CP], pltpu.roll(rows[1, BW:CP], 4, axis=0))
+    return jnp.concatenate([own, side], axis=0)
+
+
+def unpacked(block):
+    own, side = block[0 : 2 * BW].reshape(2, BW, C), block[2 * BW :]
+    sides = [jnp.where(side_places(), x, 0.0) for x in (side, pltpu.roll(side, 4, axis=0))]
+    return jnp.concatenate([own, jnp.stack(sides, 0)], axis=1)
 
 
 def from_rows(where, one, two):
@@ -176,10 +193,11 @@
     length = counts[where["section"]]
     for k in range(2):
         f = length - 2 + k
-        above, below = from_rows(where, one[f], two[f])
-        out[k, 0:2] = jnp.where(where["up"], above, jnp.zeros((2, CP, C), BF))
-        out[k, 2:6] = own[f]
-        out[k, 6:8] = jnp.where(where["down"], below, jnp.zeros((2, CP, C), BF))
+        above, below = from_rows(where, one[f].astype(F32), two[f].astype(F32))
+        out[k, 0] = jnp.where(where["up"], above, 0.0).astype(BF)
+        for r in range(2):
+            out[k, 1 + r] = packed(own[f, 2 * r : 2 * r + 2].astype(F32)).astype(BF)
+        out[k, 3] = jnp.where(where["down"], below, 0.0).astype(BF)
 
 
 def side_by_side(x, rows, cells, f):
@@ -211,8 +229,8 @@
     where = place_of(sizes)
     for f in range(F):
         above, below = from_rows(where, one[f].astype(F32), two[f].astype(F32))
-        side_by_side(jnp.where(where["up"], above, 0.0), 0, cells, f)
-        side_by_side(jnp.where(where["down"], below, 0.0), 2, cells, f)
+        side_by_side(jnp.where(where["up"], unpacked(above), 0.0), 0, cells, f)
+        side_by_side(jnp.where(where["down"], unpacked(below), 0.0), 2, cells, f)
     acc[...] = part[...]
     for dt in (2, 1, 0):
         count = F - (2 - dt)
@@ -227,11 +245,13 @@
         acc[2 - dt : F, 4 * CP : 6 * CP] += terms[2]
 
 
-def decode_kernel(sizes, counts, part, prior, weight, upw, out, mark, cells, pairs):
+def decode_kernel(sizes, counts, part, prior, weight, upw, out_hbm, mark, cells, pairs, out, sems):
     where = place_of(sizes)
     length = counts[where["section"]]
     for k in range(2):
-        side_by_side(jnp.where(where["before"], prior[k].astype(F32), 0.0), 0, cells, k)
+        for r in range(4):
+            rows = jnp.where(where["before"], unpacked(prior[k, r].astype(F32)), 0.0)
+            side_by_side(rows, 2 * r, cells, k)
 
     def term(first, count, dt):
         total = None
@@ -256,18 +276,26 @@
         pairs[1, f, :, 0:C] = hidden[CP : 5 * CP]
         pairs[1, f, :, C : 2 * C] = hidden[2 * CP : 6 * CP]
     low = lax.broadcasted_iota(jnp.int32, (1, CP, C), 2) < C // 2
-    for k in range(2):
-        rows = lax.dot_general(
+    products = [
+        lax.dot_general(
             pairs[k].reshape(F * 4 * CP, 2 * C), upw[k], NT, preferred_element_type=F32
         )
-        for f in range(F):
-            whole = rows[f * 4 * CP : (f + 1) * 4 * CP].reshape(4, CP, 2 * C)
+        for k in range(2)
+    ]
+    copies = []
+    for f in range(F):
+        for k in range(2):
+            whole = products[k][f * 4 * CP : (f + 1) * 4 * CP].reshape(4, CP, 2 * C)
             side = whole[:, :, C : 2 * C]
             mix = jnp.where(low, shifted(side, -1), shifted(side, 1))
             value = jnp.where(f < length, whole[:, :, 0:C] + mix, 0.0)[:, 0:BW].astype(BF)
             for r in range(BR):
                 out[f, 2 * r + k] = value[r]
+        copies.append(pltpu.make_async_copy(out.at[f], out_hbm.at[f], sems.at[f]))
+        copies[f].start()
     mark[...] = jnp.zeros(mark.shape, F32)
+    for copy in copies:
+        copy.wait()
 
 
 def later_group_kernel(sizes, counts, acc, later, one, two, own, total):
@@ -284,10 +312,11 @@
     own[...] = total[:, 2 * BW : 6 * BW]
 
 
-def latent_grad_kernel(sizes, counts, lat, gain, own, one, two, mark, out):
+def latent_grad_kernel(sizes, counts, lat, gain, own, one, two, mark, out_hbm, out, sems):
     where = place_of(sizes)
     length = counts[where["section"]]
     g = gain[...].reshape(1, 1, C)
+    copies = []
     for f in range(F):
         x = lat[f].astype(F32)
         above, below = from_rows(where, one[f].astype(F32), two[f].astype(F32))
@@ -301,6 +330,10 @@
         t = grad * (s + v * s * (1.0 - s)) * g
         slope = jnp.mean(t * unit, axis=-1, keepdims=True)
         out[f] = jnp.where(f < length, scale * (t - unit * slope), 0.0)
+        copies.append(pltpu.make_async_copy(out.at[f], out_hbm.at[f], sems.at[f]))
+        copies[f].start()
+    for copy in copies:
+        copy.wait()
 
 
 def call(kernel, outs, ins, scratch=(), flops=0, limit=40, outs_at=None, aliases=None):
@@ -340,7 +373,7 @@
     side = sd((2, 3 * BR * F, C), BF)
     side_one, side_two = call(kern(strips_kernel), (side, side), [VM, VM], flops=4 * 10**9)(lat, pg)
     side_one, side_two = swap(side_one, tiles, 1, 0), swap(side_two, tiles, 1, 1)
-    rim = sd((F, 2, CP, C), BF)
+    rim = sd((F, 2 * BW + 8, C), BF)
     own, one, two = call(
         kern(acts_kernel), (sd((F, BR, CP, C), BF), rim, rim), [VM, VM, VM, VM], flops=4 * 10**9
     )(lat, side_one, side_two, gain)
@@ -363,7 +396,7 @@
         flops=6 * 10**9,
     )(gh, conv_weight)
     edge = call(
-        kern(edge_frames_kernel), sd((2, 8, CP, C), BF), [SM, VM, VM, VM, ANY]
+        kern(edge_frames_kernel), sd((2, 4, 2 * BW + 8, C), BF), [SM, VM, VM, VM, ANY]
     )(counts, own, one, two, early)
     prior = ring(edge, "section", 1)
     later = ring(early, "section", -1)
@@ -397,11 +430,16 @@
         [
             pltpu.VMEM((2, 8 * CP, 3 * C), BF),
             pltpu.VMEM((2, F, 4 * CP, 2 * C), BF),
+            pltpu.VMEM((F, 2 * BR, BW, C), BF),
+            pltpu.SemaphoreType.DMA((F,)),
         ],
+        outs_at=(ANY, VM),
         flops=4 * 10**9,
     )(counts, part, prior, wide, upw)
     grad = call(
-        kern(latent_grad_kernel), sd((F, BR, BW, C), F32), [SM, VM, VM, VM, VM, VM, ANY]
+        kern(latent_grad_kernel), sd((F, BR, BW, C), F32), [SM, VM, VM, VM, VM, VM, ANY],
+        [pltpu.VMEM((F, BR, BW, C), F32), pltpu.SemaphoreType.DMA((F,))],
+        outs_at=ANY,
     )(counts, lat, gain, mine, one, two, mark)
     return (decoded[:, None], grad[:, None])
 

time: 50 us -> 49.6 us (level)
  the two profiles are of different devices: /device:TPU:1 before, /device:TPU:6 now
where the time goes in v4:
time: 49.6 us; the launch traced here: 49.1 us
  Pallas kernels  24.5 us (49%)
  starting transfers between devices  17 us (34%)
  waiting for transfers between devices  4.62 us (9%)
  local copies, waits for them, and re-layouts  2.06 us (4%)
  between operations  0.95 us (2%)
    ppermute x6, starting transfers between devices, swap(): lax.ppermute(value, 'tile', [(at, ((at + shift ^ unit) - shift) % tiles)...  14.2 us
    pallas_call x1, Pallas kernels, per_device(): call(back_kernel, (sd((F, 8 * BW, C), F32), sd((2, 8 * BW, C), BF)), [VM,...  5.91 us
    pallas_call x1, Pallas kernels, per_device(): call(kern(decode_kernel), (sd((F, 2 * BR, BW, C), BF), sd((8, 128), F32))...  5.1 us
    pallas_call x1, Pallas kernels, per_device(): call(forward_own_kernel, partial, [VM, VM, ANY], [pltpu.VMEM((F, BR * CP,...  4.04 us
    ppermute x6, waiting for transfers between devices, swap(): lax.ppermute(value, 'tile', [(at, ((at + shift ^ unit) - shift) % tiles)...  2.83 us
    pallas_call x1, Pallas kernels, per_device(): call(kern(grad_hidden_kernel), (sd((F, 6, CP, C), BF), sd((2, 2 * C, 2 *...  2.83 us
    ppermute x2, starting transfers between devices, ring(): lax.ppermute(value, axis, [(i, (i + steps) % count) for i in range(count)])  2.82 us
    pallas_call x1, Pallas kernels, per_device(): call(kern(forward_rim_kernel), partial, [VM, VM, VM, VM, ANY], [pltpu.VME...  2.57 us
  transfers between devices with their start and end apart: 8, of which 4 were waited for; matrix products, arithmetic and copies ran while one was open for 0% of the time, Pallas kernels for 45%

profile of v4, /device:TPU:6, one launch (start us, length us, event | category | flops | bytes accessed | tf_op | source)
XLA Modules:
  0.0 49.1 jit_solution(6998902809240874022)
XLA Ops:
  0.6 0.0 copy-start
  0.6 1.0 %copy-done = bf16[4,1,4,24,384]{4,3,2,1,0:T(8,128)(2,1)S(1)} copy-done((bf16[4,1,4,24,384]{4,3,2,1,0:T(8,128)(2,1)S(1)}, bf16[4,1,4,24,384]{4,3,2,1,0:T(8,128)(2,1)}, u32[]{:S(2)}) %copy-start) | copy-done | bytes 294936
  1.6 0.0 copy-start.4
  1.6 1.1 %copy-done.4 = bf16[4,1,8,24,384]{4,3,2,1,0:T(8,128)(2,1)S(1)} copy-done((bf16[4,1,8,24,384]{4,3,2,1,0:T(8,128)(2,1)S(1)}, bf16[4,1,8,24,384]{4,3,2,1,0:T(8,128)(2,1)}, u32[]{:S(2)}) %copy-start.4) | copy-done | bytes 589848
  2.7 0.0 copy-start.6
  2.7 0.0 slice-start
  2.7 0.4 shard_map.77
  3.0 7.8 %collective-permute-start = (bf16[2,48,384]{2,1,0:T(8,128)(2,1)S(1)}, bf16[2,48,384]{2,1,0:T(8,128)(2,1)S(1)}, u32[]{:S(2)}, u32[]{:S(2)}) collective-permute-start(bf16[2,48,384]{2,1,0:T(8,128)(2,1)S(1)} %get-tuple-element.16), channel_id=1, source_target_pairs={{0,63},{1,2},{2,1},{3,4},{4,3},{5,6},{6,5},{7,8},{8,7},{9,10},{10,... | collective-permute-start | bytes 221192 | tf_op jit(solution)/shard_map/ppermute | solution.py:359
  10.9 0.0 collective-permute-start.1
  10.9 0.0 copy-done.6
  10.9 0.0 copy-start.2
  10.9 0.0 copy-start.3
  10.9 0.0 copy-start.5
  10.9 0.0 slice-start.1
  10.9 2.0 %collective-permute-done.side_one.rim_one = bf16[2,48,384]{2,1,0:T(8,128)(2,1)S(1)} collective-permute-done((bf16[2,48,384]{2,1,0:T(8,128)(2,1)S(1)}, bf16[2,48,384]{2,1,0:T(8,128)(2,1)S(1)}, u32[]{:S(2)}, u32[]{:S(2)}) %collective-permute-start) | collective-permute-done | bytes 73760 | tf_op jit(solution)/shard_map/ppermute | solution.py:359
  12.9 0.0 collective-permute-done.1.side_two.rim_two
  12.9 0.5 shard_map.78
  13.4 2.6 %collective-permute-start.2 = (bf16[4,56,384]{2,1,0:T(8,128)(2,1)S(1)}, bf16[4,56,384]{2,1,0:T(8,128)(2,1)S(1)}, u32[]{:S(2)}, u32[]{:S(2)}) collective-permute-start(bf16[4,56,384]{2,1,0:T(8,128)(2,1)S(1)} %get-tuple-element.18), channel_id=1, source_target_pairs={{0,60},{1,61},{2,62},{3,7},{4,8},{5,9},{6,10},{7,3},{8,4},{9,5},{1... | collective-permute-start | bytes 516104 | tf_op jit(solution)/shard_map/ppermute | solution.py:359
  15.9 0.0 collective-permute-start.3
  15.9 0.0 copy-done.2
  15.9 0.0 copy-done.3
  16.0 0.0 copy-done.5
  16.0 2.8 %shard_map.79 = (bf16[4,6,32,384]{3,2,1,0:T(8,128)(2,1)S(1)}, bf16[2,768,768]{2,1,0:T(8,128)(2,1)S(1)}) custom-call(s32[4]{0:T(128)S(1)} %copy-done.2, bf16[4,8,24,384]{3,2,1,0:T(8,128)(2,1)S(1)} %bitcast.20, bf16[2,48,384]{2,1,0:T(8,128)(2,1)S(1)} %collective-permute-done.side_one.rim_one, bf16[2,48,384]{2,1,0:T(8,128)(2,1)S(1)} %collective-permute-done.1.side_two.rim_two, ...), custom_call_target="tpu_custom_call" | custom-call | flops 3000000000 | bytes 1000000 | tf_op jit(solution)/shard_map/pallas_call | solution.py:381
  18.8 0.0 slice-done
  18.8 0.0 slice-done.1
  18.8 5.9 %shard_map.80 = (f32[4,192,384]{2,1,0:T(8,128)S(1)}, bf16[2,192,384]{2,1,0:T(8,128)(2,1)S(1)}) custom-call(bf16[4,6,32,384]{3,2,1,0:T(8,128)(2,1)S(1)} %get-tuple-element.21.gh, bf16[3,3,3,384,384]{4,3,2,1,0:T(8,128)(2,1)S(1)} %bitcast.11), custom_call_target="tpu_custom_call" | custom-call | flops 6000000000 | bytes 1000000 | tf_op jit(solution)/shard_map/pallas_call | solution.py:388
  24.7 0.9 %collective-permute-start.4 = (bf16[2,192,384]{2,1,0:T(8,128)(2,1)S(1)}, bf16[2,192,384]{2,1,0:T(8,128)(2,1)S(1)}, u32[]{:S(2)}, u32[]{:S(2)}) collective-permute-start(bf16[2,192,384]{2,1,0:T(8,128)(2,1)S(1)} %get-tuple-element.22.early), channel_id=1, source_target_pairs={{0,192},{64,0},{128,64},{192,128},{1,193},{65,1},{129,65},{193,129... | collective-permute-start | bytes 884744 | tf_op jit(solution)/shard_map/ppermute | solution.py:354
  25.7 0.0 collective-permute-done.2.one
  25.7 0.8 %collective-permute-done.3.two = bf16[4,56,384]{2,1,0:T(8,128)(2,1)S(1)} collective-permute-done((bf16[4,56,384]{2,1,0:T(8,128)(2,1)S(1)}, bf16[4,56,384]{2,1,0:T(8,128)(2,1)S(1)}, u32[]{:S(2)}, u32[]{:S(2)}) %collective-permute-start.3) | collective-permute-done | bytes 172064 | tf_op jit(solution)/shard_map/ppermute | solution.py:359
  26.4 0.6 %shard_map.81.edge = bf16[2,4,56,384]{3,2,1,0:T(8,128)(2,1)S(1)} custom-call(s32[4]{0:T(128)S(1)} %copy-done.2, bf16[4,4,32,384]{3,2,1,0:T(8,128)(2,1)S(1)} %get-tuple-element.20.own, bf16[4,56,384]{2,1,0:T(8,128)(2,1)S(1)} %collective-permute-done.2.one, bf16[4,56,384]{2,1,0:T(8,128)(2,1)S(1)} %collective-permute-done.3.two, ...), custom_call_target="tpu_custom_call" | custom-call | bytes 1000000 | tf_op jit(solution)/shard_map/pallas_call | solution.py:398
  27.0 1.9 %collective-permute-start.5 = (bf16[2,4,56,384]{3,2,1,0:T(8,128)(2,1)S(1)}, bf16[2,4,56,384]{3,2,1,0:T(8,128)(2,1)S(1)}, u32[]{:S(2)}, u32[]{:S(2)}) collective-permute-start(bf16[2,4,56,384]{3,2,1,0:T(8,128)(2,1)S(1)} %shard_map.81.edge), channel_id=1, source_target_pairs={{0,64},{64,128},{128,192},{192,0},{1,65},{65,129},{129,193},{193,1... | collective-permute-start | bytes 1032200 | tf_op jit(solution)/shard_map/ppermute | solution.py:354
  29.0 4.0 %shard_map.82.part = f32[4,192,384]{2,1,0:T(8,128)S(1)} custom-call(bf16[4,4,32,384]{3,2,1,0:T(8,128)(2,1)S(1)} %get-tuple-element.20.own, bf16[3,3,1152,384]{3,2,1,0:T(8,128)(2,1)S(1)} %bitcast.12, bf16[2,4,56,384]{3,2,1,0:T(8,128)(2,1)S(1)} %shard_map.81.edge), custom_call_target="tpu_custom_call" | custom-call | flops 4000000000 | bytes 1000000 | tf_op jit(solution)/shard_map/pallas_call | solution.py:404
  33.0 1.8 %collective-permute-done.4.later = bf16[2,192,384]{2,1,0:T(8,128)(2,1)S(1)} collective-permute-done((bf16[2,192,384]{2,1,0:T(8,128)(2,1)S(1)}, bf16[2,192,384]{2,1,0:T(8,128)(2,1)S(1)}, u32[]{:S(2)}, u32[]{:S(2)}) %collective-permute-start.4) | collective-permute-done | bytes 294944 | tf_op jit(solution)/shard_map/ppermute | solution.py:354
  34.8 0.8 %shard_map.83 = (bf16[4,48,384]{2,1,0:T(8,128)(2,1)S(1)}, bf16[4,48,384]{2,1,0:T(8,128)(2,1)S(1)}, f32[4,96,384]{2,1,0:T(8,128)S(1)}) custom-call(s32[4]{0:T(128)S(1)} %copy-done.2, f32[4,192,384]{2,1,0:T(8,128)S(1)} %get-tuple-element.23.acc, bf16[2,192,384]{2,1,0:T(8,128)(2,1)S(1)} %collective-permute-done.4.later), custom_call_target="tpu_custom_call" | custom-call | bytes 1000000 | tf_op jit(solution)/shard_map/pallas_call | solution.py:412
  35.6 3.8 %collective-permute-start.6 = (bf16[4,48,384]{2,1,0:T(8,128)(2,1)S(1)}, bf16[4,48,384]{2,1,0:T(8,128)(2,1)S(1)}, u32[]{:S(2)}, u32[]{:S(2)}) collective-permute-start(bf16[4,48,384]{2,1,0:T(8,128)(2,1)S(1)} %get-tuple-element.27), channel_id=1, source_target_pairs={{0,60},{1,61},{2,62},{3,7},{4,8},{5,9},{6,10},{7,3},{8,4},{9,5},{1... | collective-permute-start | bytes 442376 | tf_op jit(solution)/shard_map/ppermute | solution.py:359
  39.4 0.0 collective-permute-start.7
  39.4 2.6 %shard_map.84.part = f32[4,192,384]{2,1,0:T(8,128)S(1)} custom-call(bf16[4,56,384]{2,1,0:T(8,128)(2,1)S(1)} %collective-permute-done.2.one, bf16[4,56,384]{2,1,0:T(8,128)(2,1)S(1)} %collective-permute-done.3.two, f32[4,192,384]{2,1,0:T(8,128)S(1)} %shard_map.82.part, bf16[3,3,1152,384]{3,2,1,0:T(8,128)(2,1)S(1)} %bitcast.13, ...), custom_call_target="tpu_custom_call" | custom-call | flops 3000000000 | bytes 1000000 | tf_op jit(solution)/shard_map/pallas_call | solution.py:419
  41.9 0.0 collective-permute-done.5.prior
  42.0 0.0 copy-start.1
  42.0 5.1 %shard_map.85 = (bf16[4,8,24,384]{3,2,1,0:T(8,128)(2,1)}, f32[8,128]{1,0:T(8,128)S(1)}) custom-call(s32[4]{0:T(128)S(1)} %copy-done.2, f32[4,192,384]{2,1,0:T(8,128)S(1)} %shard_map.84.part, bf16[2,4,56,384]{3,2,1,0:T(8,128)(2,1)S(1)} %collective-permute-done.5.prior, bf16[3,3,1152,384]{3,2,1,0:T(8,128)(2,1)S(1)} %bitcast.14, ...), custom_call_target="tpu_custom_call" | custom-call | flops 4000000000 | bytes 1000000 | tf_op jit(solution)/shard_map/pallas_call | solution.py:426
  47.1 0.0 collective-permute-done.6.one
  47.1 0.1 collective-permute-done.7.two
  47.2 0.0 copy-done.1
  47.2 1.8 %shard_map.86 = f32[4,4,24,384]{3,2,1,0:T(8,128)} custom-call(s32[4]{0:T(128)S(1)} %copy-done.2, bf16[4,4,24,384]{3,2,1,0:T(8,128)(2,1)S(1)} %bitcast.17, f32[1,384]{1,0:T(1,128)S(1)} %reshape.10.gain, f32[4,96,384]{2,1,0:T(8,128)S(1)} %get-tuple-element.24.mine.own, bf16[4,48,384]{2,1,0:T(8,128)(2,1)S(1)} %collective-permute-done.6.one, ...), custom_call_target="tpu_custom_call" | custom-call | bytes 1000000 | tf_op jit(solution)/shard_map/pallas_call | solution.py:439
  (2 shorter events, 0.0 us)
Async XLA Ops:
  0.6 1.0 %copy-start = (bf16[4,1,4,24,384]{4,3,2,1,0:T(8,128)(2,1)S(1)}, bf16[4,1,4,24,384]{4,3,2,1,0:T(8,128)(2,1)}, u32[]{:S(2)}) copy-start(bf16[4,1,4,24,384]{4,3,2,1,0:T(8,128)(2,1)} %param.6) | copy-start | bytes 884740
  1.6 1.1 %copy-start.4 = (bf16[4,1,8,24,384]{4,3,2,1,0:T(8,128)(2,1)S(1)}, bf16[4,1,8,24,384]{4,3,2,1,0:T(8,128)(2,1)}, u32[]{:S(2)}) copy-start(bf16[4,1,8,24,384]{4,3,2,1,0:T(8,128)(2,1)} %param.11) | copy-start | bytes 1769476
  2.7 8.2 %copy-start.6 = (f32[384]{0:T(512)S(1)}, f32[384]{0:T(512)}, u32[]{:S(2)}) copy-start(f32[384]{0:T(512)} %param.8) | copy-start | bytes 4612
  2.7 16.1 %slice-start = ((s8[7962624]{0:T(1024)(128)(4,1)}), s8[4194304]{0:T(1024)(128)(4,1)S(1)}, s32[]{:S(2)}) async-start(s8[7962624]{0:T(1024)(128)(4,1)} %bitcast.10), calls=%async_computation | async-start | bytes 8388608
  3.0 9.9 %collective-permute-start = (bf16[2,48,384]{2,1,0:T(8,128)(2,1)S(1)}, bf16[2,48,384]{2,1,0:T(8,128)(2,1)S(1)}, u32[]{:S(2)}, u32[]{:S(2)}) collective-permute-start(bf16[2,48,384]{2,1,0:T(8,128)(2,1)S(1)} %get-tuple-element.16), channel_id=1, source_target_pairs={{0,63},{1,2},{2,1},{3,4},{4,3},{5,6},{6,5},{7,8},{8,7},{9,10},{10,... | collective-permute-start | bytes 221192 | tf_op jit(solution)/shard_map/ppermute | solution.py:359
  10.9 2.0 %collective-permute-start.1 = (bf16[2,48,384]{2,1,0:T(8,128)(2,1)S(1)}, bf16[2,48,384]{2,1,0:T(8,128)(2,1)S(1)}, u32[]{:S(2)}, u32[]{:S(2)}) collective-permute-start(bf16[2,48,384]{2,1,0:T(8,128)(2,1)S(1)} %get-tuple-element.17), channel_id=1, source_target_pairs={{0,1},{1,0},{2,3},{3,2},{4,5},{5,4},{6,7},{7,6},{8,9},{9,8},{10,11... | collective-permute-start | bytes 221192 | tf_op jit(solution)/shard_map/ppermute | solution.py:359
  10.9 5.1 %copy-start.2 = (s32[4]{0:T(128)S(1)}, s32[4]{0:T(128)}, u32[]{:S(2)}) copy-start(s32[4]{0:T(128)} %counts.9) | copy-start | bytes 52
  10.9 5.1 %copy-start.3 = (bf16[3,3,384,192]{2,3,1,0:T(8,128)(2,1)S(1)}, bf16[3,3,384,192]{2,3,1,0:T(8,128)(2,1)}, u32[]{:S(2)}) copy-start(bf16[3,3,384,192]{2,3,1,0:T(8,128)(2,1)} %param.10) | copy-start | bytes 3981316
  10.9 5.1 %copy-start.5 = (bf16[4,1,8,24,384]{4,3,2,1,0:T(8,128)(2,1)S(1)}, bf16[4,1,8,24,384]{4,3,2,1,0:T(8,128)(2,1)}, u32[]{:S(2)}) copy-start(bf16[4,1,8,24,384]{4,3,2,1,0:T(8,128)(2,1)} %param.11) | copy-start | bytes 1769476
  10.9 7.9 %slice-start.1 = ((s8[7962624]{0:T(1024)(128)(4,1)}), s8[3768320]{0:T(1024)(128)(4,1)S(1)}, s32[]{:S(2)}) async-start(s8[7962624]{0:T(1024)(128)(4,1)} %bitcast.10), calls=%async_computation.1 | async-start | bytes 7536640
  13.4 12.3 %collective-permute-start.2 = (bf16[4,56,384]{2,1,0:T(8,128)(2,1)S(1)}, bf16[4,56,384]{2,1,0:T(8,128)(2,1)S(1)}, u32[]{:S(2)}, u32[]{:S(2)}) collective-permute-start(bf16[4,56,384]{2,1,0:T(8,128)(2,1)S(1)} %get-tuple-element.18), channel_id=1, source_target_pairs={{0,60},{1,61},{2,62},{3,7},{4,8},{5,9},{6,10},{7,3},{8,4},{9,5},{1... | collective-permute-start | bytes 516104 | tf_op jit(solution)/shard_map/ppermute | solution.py:359
  15.9 10.5 %collective-permute-start.3 = (bf16[4,56,384]{2,1,0:T(8,128)(2,1)S(1)}, bf16[4,56,384]{2,1,0:T(8,128)(2,1)S(1)}, u32[]{:S(2)}, u32[]{:S(2)}) collective-permute-start(bf16[4,56,384]{2,1,0:T(8,128)(2,1)S(1)} %get-tuple-element.19), channel_id=1, source_target_pairs={{0,4},{1,5},{2,6},{3,63},{4,0},{5,1},{6,2},{7,11},{8,12},{9,13},{1... | collective-permute-start | bytes 516104 | tf_op jit(solution)/shard_map/ppermute | solution.py:359
  24.7 10.0 %collective-permute-start.4 = (bf16[2,192,384]{2,1,0:T(8,128)(2,1)S(1)}, bf16[2,192,384]{2,1,0:T(8,128)(2,1)S(1)}, u32[]{:S(2)}, u32[]{:S(2)}) collective-permute-start(bf16[2,192,384]{2,1,0:T(8,128)(2,1)S(1)} %get-tuple-element.22.early), channel_id=1, source_target_pairs={{0,192},{64,0},{128,64},{192,128},{1,193},{65,1},{129,65},{193,129... | collective-permute-start | bytes 884744 | tf_op jit(solution)/shard_map/ppermute | solution.py:354
  27.0 14.9 %collective-permute-start.5 = (bf16[2,4,56,384]{3,2,1,0:T(8,128)(2,1)S(1)}, bf16[2,4,56,384]{3,2,1,0:T(8,128)(2,1)S(1)}, u32[]{:S(2)}, u32[]{:S(2)}) collective-permute-start(bf16[2,4,56,384]{3,2,1,0:T(8,128)(2,1)S(1)} %shard_map.81.edge), channel_id=1, source_target_pairs={{0,64},{64,128},{128,192},{192,0},{1,65},{65,129},{129,193},{193,1... | collective-permute-start | bytes 1032200 | tf_op jit(solution)/shard_map/ppermute | solution.py:354
  35.6 11.5 %collective-permute-start.6 = (bf16[4,48,384]{2,1,0:T(8,128)(2,1)S(1)}, bf16[4,48,384]{2,1,0:T(8,128)(2,1)S(1)}, u32[]{:S(2)}, u32[]{:S(2)}) collective-permute-start(bf16[4,48,384]{2,1,0:T(8,128)(2,1)S(1)} %get-tuple-element.27), channel_id=1, source_target_pairs={{0,60},{1,61},{2,62},{3,7},{4,8},{5,9},{6,10},{7,3},{8,4},{9,5},{1... | collective-permute-start | bytes 442376 | tf_op jit(solution)/shard_map/ppermute | solution.py:359
  39.4 7.8 %collective-permute-start.7 = (bf16[4,48,384]{2,1,0:T(8,128)(2,1)S(1)}, bf16[4,48,384]{2,1,0:T(8,128)(2,1)S(1)}, u32[]{:S(2)}, u32[]{:S(2)}) collective-permute-start(bf16[4,48,384]{2,1,0:T(8,128)(2,1)S(1)} %get-tuple-element.28), channel_id=1, source_target_pairs={{0,4},{1,5},{2,6},{3,63},{4,0},{5,1},{6,2},{7,11},{8,12},{9,13},{1... | collective-permute-start | bytes 442376 | tf_op jit(solution)/shard_map/ppermute | solution.py:359
  42.0 5.2 %copy-start.1 = (bf16[4,1,4,24,384]{4,3,2,1,0:T(8,128)(2,1)S(1)}, bf16[4,1,4,24,384]{4,3,2,1,0:T(8,128)(2,1)}, u32[]{:S(2)}) copy-start(bf16[4,1,4,24,384]{4,3,2,1,0:T(8,128)(2,1)} %param.6) | copy-start | bytes 884740

commit v5 on v4

--- a/solution.py
+++ b/solution.py
@@ -298,18 +298,18 @@
         copy.wait()
 
 
-def later_group_kernel(sizes, counts, acc, later, one, two, own, total):
-    where = place_of(sizes)
-    length = counts[where["section"]]
-    total[...] = acc[...]
-    for k in range(2):
-        f = length - 2 + k
-        total[f] += jnp.where(where["after"], later[k].astype(F32), 0.0)
-    top, bottom = total[:, 0 : 2 * BW], total[:, 6 * BW : 8 * BW]
+def later_group_kernel(sizes, counts, acc, later, one, two, own):
+    where = place_of(sizes)
+    length = jnp.where(where["after"], counts[where["section"]], -8)
     below = where["first_below"]
-    one[...] = jnp.where(below, bottom, top).astype(BF)
-    two[...] = jnp.where(below, top, bottom).astype(BF)
-    own[...] = total[:, 2 * BW : 6 * BW]
+    for f in range(F):
+        total = acc[f]
+        for k in range(2):
+            total = total + jnp.where(f == length - 2 + k, later[k].astype(F32), 0.0)
+        top, bottom = total[0 : 2 * BW], total[6 * BW : 8 * BW]
+        one[f] = jnp.where(below, bottom, top).astype(BF)
+        two[f] = jnp.where(below, top, bottom).astype(BF)
+        own[f] = total[2 * BW : 6 * BW]
 
 
 def latent_grad_kernel(sizes, counts, lat, gain, own, one, two, mark, out_hbm, out, sems):
@@ -413,7 +413,6 @@
         kern(later_group_kernel),
         (sd((F, 2 * BW, C), BF), sd((F, 2 * BW, C), BF), sd((F, 4 * BW, C), F32)),
         [SM, VM, VM],
-        [pltpu.VMEM((F, 8 * BW, C), F32)],
     )(counts, acc, later)
     one, two = swap(one, tiles, GCOL, 0), swap(two, tiles, GCOL, 1)
     part = call(

time: 49.6 us -> 49.6 us (level)
  no operation moved by 1% of the time
where the time goes in v5:
time: 49.6 us; the launch traced here: 49.2 us
  Pallas kernels  24.5 us (49%)
  starting transfers between devices  17 us (34%)
  waiting for transfers between devices  4.62 us (9%)
  local copies, waits for them, and re-layouts  2.06 us (4%)
  between operations  0.95 us (2%)
    ppermute x6, starting transfers between devices, swap(): lax.ppermute(value, 'tile', [(at, ((at + shift ^ unit) - shift) % tiles)...  14.2 us
    pallas_call x1, Pallas kernels, per_device(): call(back_kernel, (sd((F, 8 * BW, C), F32), sd((2, 8 * BW, C), BF)), [VM,...  5.91 us
    pallas_call x1, Pallas kernels, per_device(): call(kern(decode_kernel), (sd((F, 2 * BR, BW, C), BF), sd((8, 128), F32))...  5.1 us
    pallas_call x1, Pallas kernels, per_device(): call(forward_own_kernel, partial, [VM, VM, ANY], [pltpu.VMEM((F, BR * CP,...  4.04 us
    ppermute x6, waiting for transfers between devices, swap(): lax.ppermute(value, 'tile', [(at, ((at + shift ^ unit) - shift) % tiles)...  2.83 us
    pallas_call x1, Pallas kernels, per_device(): call(kern(grad_hidden_kernel), (sd((F, 6, CP, C), BF), sd((2, 2 * C, 2 *...  2.83 us
    ppermute x2, starting transfers between devices, ring(): lax.ppermute(value, axis, [(i, (i + steps) % count) for i in range(count)])  2.82 us
    pallas_call x1, Pallas kernels, per_device(): call(kern(forward_rim_kernel), partial, [VM, VM, VM, VM, ANY], [pltpu.VME...  2.57 us
  transfers between devices with their start and end apart: 8, of which 4 were waited for; matrix products, arithmetic and copies ran while one was open for 0% of the time, Pallas kernels for 45%

profile of v5, /device:TPU:6, one launch (start us, length us, event | category | flops | bytes accessed | tf_op | source)
XLA Modules:
  0.0 49.2 jit_solution(11214664575179467432)
XLA Ops:
  0.6 0.0 copy-start
  0.6 1.0 %copy-done = bf16[4,1,4,24,384]{4,3,2,1,0:T(8,128)(2,1)S(1)} copy-done((bf16[4,1,4,24,384]{4,3,2,1,0:T(8,128)(2,1)S(1)}, bf16[4,1,4,24,384]{4,3,2,1,0:T(8,128)(2,1)}, u32[]{:S(2)}) %copy-start) | copy-done | bytes 294936
  1.6 0.0 copy-start.4
  1.6 1.1 %copy-done.4 = bf16[4,1,8,24,384]{4,3,2,1,0:T(8,128)(2,1)S(1)} copy-done((bf16[4,1,8,24,384]{4,3,2,1,0:T(8,128)(2,1)S(1)}, bf16[4,1,8,24,384]{4,3,2,1,0:T(8,128)(2,1)}, u32[]{:S(2)}) %copy-start.4) | copy-done | bytes 589848
  2.7 0.0 copy-start.6
  2.7 0.0 slice-start
  2.7 0.4 shard_map.77
  3.0 7.8 %collective-permute-start = (bf16[2,48,384]{2,1,0:T(8,128)(2,1)S(1)}, bf16[2,48,384]{2,1,0:T(8,128)(2,1)S(1)}, u32[]{:S(2)}, u32[]{:S(2)}) collective-permute-start(bf16[2,48,384]{2,1,0:T(8,128)(2,1)S(1)} %get-tuple-element.16), channel_id=1, source_target_pairs={{0,63},{1,2},{2,1},{3,4},{4,3},{5,6},{6,5},{7,8},{8,7},{9,10},{10,... | collective-permute-start | bytes 221192 | tf_op jit(solution)/shard_map/ppermute | solution.py:359
  10.9 0.0 collective-permute-start.1
  10.9 0.0 copy-done.6
  10.9 0.0 copy-start.2
  10.9 0.0 copy-start.3
  10.9 0.0 copy-start.5
  10.9 0.0 slice-start.1
  10.9 2.0 %collective-permute-done.side_one.rim_one = bf16[2,48,384]{2,1,0:T(8,128)(2,1)S(1)} collective-permute-done((bf16[2,48,384]{2,1,0:T(8,128)(2,1)S(1)}, bf16[2,48,384]{2,1,0:T(8,128)(2,1)S(1)}, u32[]{:S(2)}, u32[]{:S(2)}) %collective-permute-start) | collective-permute-done | bytes 73760 | tf_op jit(solution)/shard_map/ppermute | solution.py:359
  12.9 0.0 collective-permute-done.1.side_two.rim_two
  12.9 0.5 shard_map.78
  13.4 2.6 %collective-permute-start.2 = (bf16[4,56,384]{2,1,0:T(8,128)(2,1)S(1)}, bf16[4,56,384]{2,1,0:T(8,128)(2,1)S(1)}, u32[]{:S(2)}, u32[]{:S(2)}) collective-permute-start(bf16[4,56,384]{2,1,0:T(8,128)(2,1)S(1)} %get-tuple-element.18), channel_id=1, source_target_pairs={{0,60},{1,61},{2,62},{3,7},{4,8},{5,9},{6,10},{7,3},{8,4},{9,5},{1... | collective-permute-start | bytes 516104 | tf_op jit(solution)/shard_map/ppermute | solution.py:359
  15.9 0.0 collective-permute-start.3
  15.9 0.0 copy-done.2
  15.9 0.0 copy-done.3
  16.0 0.0 copy-done.5
  16.0 2.8 %shard_map.79 = (bf16[4,6,32,384]{3,2,1,0:T(8,128)(2,1)S(1)}, bf16[2,768,768]{2,1,0:T(8,128)(2,1)S(1)}) custom-call(s32[4]{0:T(128)S(1)} %copy-done.2, bf16[4,8,24,384]{3,2,1,0:T(8,128)(2,1)S(1)} %bitcast.20, bf16[2,48,384]{2,1,0:T(8,128)(2,1)S(1)} %collective-permute-done.side_one.rim_one, bf16[2,48,384]{2,1,0:T(8,128)(2,1)S(1)} %collective-permute-done.1.side_two.rim_two, ...), custom_call_target="tpu_custom_call" | custom-call | flops 3000000000 | bytes 1000000 | tf_op jit(solution)/shard_map/pallas_call | solution.py:381
  18.8 0.0 slice-done
  18.8 0.0 slice-done.1
  18.8 5.9 %shard_map.80 = (f32[4,192,384]{2,1,0:T(8,128)S(1)}, bf16[2,192,384]{2,1,0:T(8,128)(2,1)S(1)}) custom-call(bf16[4,6,32,384]{3,2,1,0:T(8,128)(2,1)S(1)} %get-tuple-element.21.gh, bf16[3,3,3,384,384]{4,3,2,1,0:T(8,128)(2,1)S(1)} %bitcast.11), custom_call_target="tpu_custom_call" | custom-call | flops 6000000000 | bytes 1000000 | tf_op jit(solution)/shard_map/pallas_call | solution.py:388
  24.7 0.9 %collective-permute-start.4 = (bf16[2,192,384]{2,1,0:T(8,128)(2,1)S(1)}, bf16[2,192,384]{2,1,0:T(8,128)(2,1)S(1)}, u32[]{:S(2)}, u32[]{:S(2)}) collective-permute-start(bf16[2,192,384]{2,1,0:T(8,128)(2,1)S(1)} %get-tuple-element.22.early), channel_id=1, source_target_pairs={{0,192},{64,0},{128,64},{192,128},{1,193},{65,1},{129,65},{193,129... | collective-permute-start | bytes 884744 | tf_op jit(solution)/shard_map/ppermute | solution.py:354
  25.7 0.0 collective-permute-done.2.one
  25.7 0.8 %collective-permute-done.3.two = bf16[4,56,384]{2,1,0:T(8,128)(2,1)S(1)} collective-permute-done((bf16[4,56,384]{2,1,0:T(8,128)(2,1)S(1)}, bf16[4,56,384]{2,1,0:T(8,128)(2,1)S(1)}, u32[]{:S(2)}, u32[]{:S(2)}) %collective-permute-start.3) | collective-permute-done | bytes 172064 | tf_op jit(solution)/shard_map/ppermute | solution.py:359
  26.4 0.6 %shard_map.81.edge = bf16[2,4,56,384]{3,2,1,0:T(8,128)(2,1)S(1)} custom-call(s32[4]{0:T(128)S(1)} %copy-done.2, bf16[4,4,32,384]{3,2,1,0:T(8,128)(2,1)S(1)} %get-tuple-element.20.own, bf16[4,56,384]{2,1,0:T(8,128)(2,1)S(1)} %collective-permute-done.2.one, bf16[4,56,384]{2,1,0:T(8,128)(2,1)S(1)} %collective-permute-done.3.two, ...), custom_call_target="tpu_custom_call" | custom-call | bytes 1000000 | tf_op jit(solution)/shard_map/pallas_call | solution.py:398
  27.0 1.9 %collective-permute-start.5 = (bf16[2,4,56,384]{3,2,1,0:T(8,128)(2,1)S(1)}, bf16[2,4,56,384]{3,2,1,0:T(8,128)(2,1)S(1)}, u32[]{:S(2)}, u32[]{:S(2)}) collective-permute-start(bf16[2,4,56,384]{3,2,1,0:T(8,128)(2,1)S(1)} %shard_map.81.edge), channel_id=1, source_target_pairs={{0,64},{64,128},{128,192},{192,0},{1,65},{65,129},{129,193},{193,1... | collective-permute-start | bytes 1032200 | tf_op jit(solution)/shard_map/ppermute | solution.py:354
  29.0 4.0 %shard_map.82.part = f32[4,192,384]{2,1,0:T(8,128)S(1)} custom-call(bf16[4,4,32,384]{3,2,1,0:T(8,128)(2,1)S(1)} %get-tuple-element.20.own, bf16[3,3,1152,384]{3,2,1,0:T(8,128)(2,1)S(1)} %bitcast.12, bf16[2,4,56,384]{3,2,1,0:T(8,128)(2,1)S(1)} %shard_map.81.edge), custom_call_target="tpu_custom_call" | custom-call | flops 4000000000 | bytes 1000000 | tf_op jit(solution)/shard_map/pallas_call | solution.py:404
  33.0 1.8 %collective-permute-done.4.later = bf16[2,192,384]{2,1,0:T(8,128)(2,1)S(1)} collective-permute-done((bf16[2,192,384]{2,1,0:T(8,128)(2,1)S(1)}, bf16[2,192,384]{2,1,0:T(8,128)(2,1)S(1)}, u32[]{:S(2)}, u32[]{:S(2)}) %collective-permute-start.4) | collective-permute-done | bytes 294944 | tf_op jit(solution)/shard_map/ppermute | solution.py:354
  34.8 0.8 %shard_map.83 = (bf16[4,48,384]{2,1,0:T(8,128)(2,1)S(1)}, bf16[4,48,384]{2,1,0:T(8,128)(2,1)S(1)}, f32[4,96,384]{2,1,0:T(8,128)S(1)}) custom-call(s32[4]{0:T(128)S(1)} %copy-done.2, f32[4,192,384]{2,1,0:T(8,128)S(1)} %get-tuple-element.23.acc, bf16[2,192,384]{2,1,0:T(8,128)(2,1)S(1)} %collective-permute-done.4.later), custom_call_target="tpu_custom_call" | custom-call | bytes 1000000 | tf_op jit(solution)/shard_map/pallas_call | solution.py:412
  35.6 3.8 %collective-permute-start.6 = (bf16[4,48,384]{2,1,0:T(8,128)(2,1)S(1)}, bf16[4,48,384]{2,1,0:T(8,128)(2,1)S(1)}, u32[]{:S(2)}, u32[]{:S(2)}) collective-permute-start(bf16[4,48,384]{2,1,0:T(8,128)(2,1)S(1)} %get-tuple-element.27), channel_id=1, source_target_pairs={{0,60},{1,61},{2,62},{3,7},{4,8},{5,9},{6,10},{7,3},{8,4},{9,5},{1... | collective-permute-start | bytes 442376 | tf_op jit(solution)/shard_map/ppermute | solution.py:359
  39.4 0.0 collective-permute-start.7
  39.4 2.6 %shard_map.84.part = f32[4,192,384]{2,1,0:T(8,128)S(1)} custom-call(bf16[4,56,384]{2,1,0:T(8,128)(2,1)S(1)} %collective-permute-done.2.one, bf16[4,56,384]{2,1,0:T(8,128)(2,1)S(1)} %collective-permute-done.3.two, f32[4,192,384]{2,1,0:T(8,128)S(1)} %shard_map.82.part, bf16[3,3,1152,384]{3,2,1,0:T(8,128)(2,1)S(1)} %bitcast.13, ...), custom_call_target="tpu_custom_call" | custom-call | flops 3000000000 | bytes 1000000 | tf_op jit(solution)/shard_map/pallas_call | solution.py:418
  42.0 0.0 collective-permute-done.5.prior
  42.0 0.0 copy-start.1
  42.0 5.1 %shard_map.85 = (bf16[4,8,24,384]{3,2,1,0:T(8,128)(2,1)}, f32[8,128]{1,0:T(8,128)S(1)}) custom-call(s32[4]{0:T(128)S(1)} %copy-done.2, f32[4,192,384]{2,1,0:T(8,128)S(1)} %shard_map.84.part, bf16[2,4,56,384]{3,2,1,0:T(8,128)(2,1)S(1)} %collective-permute-done.5.prior, bf16[3,3,1152,384]{3,2,1,0:T(8,128)(2,1)S(1)} %bitcast.14, ...), custom_call_target="tpu_custom_call" | custom-call | flops 4000000000 | bytes 1000000 | tf_op jit(solution)/shard_map/pallas_call | solution.py:425
  47.1 0.0 collective-permute-done.6.one
  47.1 0.1 collective-permute-done.7.two
  47.2 0.0 copy-done.1
  47.2 1.8 %shard_map.86 = f32[4,4,24,384]{3,2,1,0:T(8,128)} custom-call(s32[4]{0:T(128)S(1)} %copy-done.2, bf16[4,4,24,384]{3,2,1,0:T(8,128)(2,1)S(1)} %bitcast.17, f32[1,384]{1,0:T(1,128)S(1)} %reshape.10.gain, f32[4,96,384]{2,1,0:T(8,128)S(1)} %get-tuple-element.24.mine.own, bf16[4,48,384]{2,1,0:T(8,128)(2,1)S(1)} %collective-permute-done.6.one, ...), custom_call_target="tpu_custom_call" | custom-call | bytes 1000000 | tf_op jit(solution)/shard_map/pallas_call | solution.py:438
  (2 shorter events, 0.0 us)
Async XLA Ops:
  0.6 1.0 %copy-start = (bf16[4,1,4,24,384]{4,3,2,1,0:T(8,128)(2,1)S(1)}, bf16[4,1,4,24,384]{4,3,2,1,0:T(8,128)(2,1)}, u32[]{:S(2)}) copy-start(bf16[4,1,4,24,384]{4,3,2,1,0:T(8,128)(2,1)} %param.6) | copy-start | bytes 884740
  1.6 1.1 %copy-start.4 = (bf16[4,1,8,24,384]{4,3,2,1,0:T(8,128)(2,1)S(1)}, bf16[4,1,8,24,384]{4,3,2,1,0:T(8,128)(2,1)}, u32[]{:S(2)}) copy-start(bf16[4,1,8,24,384]{4,3,2,1,0:T(8,128)(2,1)} %param.11) | copy-start | bytes 1769476
  2.7 8.2 %copy-start.6 = (f32[384]{0:T(512)S(1)}, f32[384]{0:T(512)}, u32[]{:S(2)}) copy-start(f32[384]{0:T(512)} %param.8) | copy-start | bytes 4612
  2.7 16.1 %slice-start = ((s8[7962624]{0:T(1024)(128)(4,1)}), s8[4194304]{0:T(1024)(128)(4,1)S(1)}, s32[]{:S(2)}) async-start(s8[7962624]{0:T(1024)(128)(4,1)} %bitcast.10), calls=%async_computation | async-start | bytes 8388608
  3.0 9.9 %collective-permute-start = (bf16[2,48,384]{2,1,0:T(8,128)(2,1)S(1)}, bf16[2,48,384]{2,1,0:T(8,128)(2,1)S(1)}, u32[]{:S(2)}, u32[]{:S(2)}) collective-permute-start(bf16[2,48,384]{2,1,0:T(8,128)(2,1)S(1)} %get-tuple-element.16), channel_id=1, source_target_pairs={{0,63},{1,2},{2,1},{3,4},{4,3},{5,6},{6,5},{7,8},{8,7},{9,10},{10,... | collective-permute-start | bytes 221192 | tf_op jit(solution)/shard_map/ppermute | solution.py:359
  10.9 2.0 %collective-permute-start.1 = (bf16[2,48,384]{2,1,0:T(8,128)(2,1)S(1)}, bf16[2,48,384]{2,1,0:T(8,128)(2,1)S(1)}, u32[]{:S(2)}, u32[]{:S(2)}) collective-permute-start(bf16[2,48,384]{2,1,0:T(8,128)(2,1)S(1)} %get-tuple-element.17), channel_id=1, source_target_pairs={{0,1},{1,0},{2,3},{3,2},{4,5},{5,4},{6,7},{7,6},{8,9},{9,8},{10,11... | collective-permute-start | bytes 221192 | tf_op jit(solution)/shard_map/ppermute | solution.py:359
  10.9 5.1 %copy-start.2 = (s32[4]{0:T(128)S(1)}, s32[4]{0:T(128)}, u32[]{:S(2)}) copy-start(s32[4]{0:T(128)} %counts.9) | copy-start | bytes 52
  10.9 5.1 %copy-start.3 = (bf16[3,3,384,192]{2,3,1,0:T(8,128)(2,1)S(1)}, bf16[3,3,384,192]{2,3,1,0:T(8,128)(2,1)}, u32[]{:S(2)}) copy-start(bf16[3,3,384,192]{2,3,1,0:T(8,128)(2,1)} %param.10) | copy-start | bytes 3981316
  10.9 5.1 %copy-start.5 = (bf16[4,1,8,24,384]{4,3,2,1,0:T(8,128)(2,1)S(1)}, bf16[4,1,8,24,384]{4,3,2,1,0:T(8,128)(2,1)}, u32[]{:S(2)}) copy-start(bf16[4,1,8,24,384]{4,3,2,1,0:T(8,128)(2,1)} %param.11) | copy-start | bytes 1769476
  10.9 7.9 %slice-start.1 = ((s8[7962624]{0:T(1024)(128)(4,1)}), s8[3768320]{0:T(1024)(128)(4,1)S(1)}, s32[]{:S(2)}) async-start(s8[7962624]{0:T(1024)(128)(4,1)} %bitcast.10), calls=%async_computation.1 | async-start | bytes 7536640
  13.4 12.3 %collective-permute-start.2 = (bf16[4,56,384]{2,1,0:T(8,128)(2,1)S(1)}, bf16[4,56,384]{2,1,0:T(8,128)(2,1)S(1)}, u32[]{:S(2)}, u32[]{:S(2)}) collective-permute-start(bf16[4,56,384]{2,1,0:T(8,128)(2,1)S(1)} %get-tuple-element.18), channel_id=1, source_target_pairs={{0,60},{1,61},{2,62},{3,7},{4,8},{5,9},{6,10},{7,3},{8,4},{9,5},{1... | collective-permute-start | bytes 516104 | tf_op jit(solution)/shard_map/ppermute | solution.py:359
  15.9 10.5 %collective-permute-start.3 = (bf16[4,56,384]{2,1,0:T(8,128)(2,1)S(1)}, bf16[4,56,384]{2,1,0:T(8,128)(2,1)S(1)}, u32[]{:S(2)}, u32[]{:S(2)}) collective-permute-start(bf16[4,56,384]{2,1,0:T(8,128)(2,1)S(1)} %get-tuple-element.19), channel_id=1, source_target_pairs={{0,4},{1,5},{2,6},{3,63},{4,0},{5,1},{6,2},{7,11},{8,12},{9,13},{1... | collective-permute-start | bytes 516104 | tf_op jit(solution)/shard_map/ppermute | solution.py:359
  24.7 10.0 %collective-permute-start.4 = (bf16[2,192,384]{2,1,0:T(8,128)(2,1)S(1)}, bf16[2,192,384]{2,1,0:T(8,128)(2,1)S(1)}, u32[]{:S(2)}, u32[]{:S(2)}) collective-permute-start(bf16[2,192,384]{2,1,0:T(8,128)(2,1)S(1)} %get-tuple-element.22.early), channel_id=1, source_target_pairs={{0,192},{64,0},{128,64},{192,128},{1,193},{65,1},{129,65},{193,129... | collective-permute-start | bytes 884744 | tf_op jit(solution)/shard_map/ppermute | solution.py:354
  27.0 14.9 %collective-permute-start.5 = (bf16[2,4,56,384]{3,2,1,0:T(8,128)(2,1)S(1)}, bf16[2,4,56,384]{3,2,1,0:T(8,128)(2,1)S(1)}, u32[]{:S(2)}, u32[]{:S(2)}) collective-permute-start(bf16[2,4,56,384]{3,2,1,0:T(8,128)(2,1)S(1)} %shard_map.81.edge), channel_id=1, source_target_pairs={{0,64},{64,128},{128,192},{192,0},{1,65},{65,129},{129,193},{193,1... | collective-permute-start | bytes 1032200 | tf_op jit(solution)/shard_map/ppermute | solution.py:354
  35.6 11.5 %collective-permute-start.6 = (bf16[4,48,384]{2,1,0:T(8,128)(2,1)S(1)}, bf16[4,48,384]{2,1,0:T(8,128)(2,1)S(1)}, u32[]{:S(2)}, u32[]{:S(2)}) collective-permute-start(bf16[4,48,384]{2,1,0:T(8,128)(2,1)S(1)} %get-tuple-element.27), channel_id=1, source_target_pairs={{0,60},{1,61},{2,62},{3,7},{4,8},{5,9},{6,10},{7,3},{8,4},{9,5},{1... | collective-permute-start | bytes 442376 | tf_op jit(solution)/shard_map/ppermute | solution.py:359
  39.4 7.8 %collective-permute-start.7 = (bf16[4,48,384]{2,1,0:T(8,128)(2,1)S(1)}, bf16[4,48,384]{2,1,0:T(8,128)(2,1)S(1)}, u32[]{:S(2)}, u32[]{:S(2)}) collective-permute-start(bf16[4,48,384]{2,1,0:T(8,128)(2,1)S(1)} %get-tuple-element.28), channel_id=1, source_target_pairs={{0,4},{1,5},{2,6},{3,63},{4,0},{5,1},{6,2},{7,11},{8,12},{9,13},{1... | collective-permute-start | bytes 442376 | tf_op jit(solution)/shard_map/ppermute | solution.py:359
  42.0 5.2 %copy-start.1 = (bf16[4,1,4,24,384]{4,3,2,1,0:T(8,128)(2,1)S(1)}, bf16[4,1,4,24,384]{4,3,2,1,0:T(8,128)(2,1)}, u32[]{:S(2)}) copy-start(bf16[4,1,4,24,384]{4,3,2,1,0:T(8,128)(2,1)} %param.6) | copy-start | bytes 884740
